TPU v7x, 256 devices: a whole 4x4x8 slice. The times are simulated.
256 devices in a mesh: seq: 32 (over z_lo, y, core), tp: 8 (over x, z_hi).
Axes of the slice: x: 4, y: 4, z: 8 (z_hi: 2, z_lo: 4; z = z_hi * 4 + z_lo), core: 2. Of those that a mesh axis runs over, the one named last changes fastest.
Arguments:
- q_prefill: bfloat16 [2, 8192, 8, 512], P(None, 'seq', 'tp'), may hold values from -6 to 6
- kv_prefill: bfloat16 [2, 8192, 8, 256], P(None, 'seq', 'tp'), may hold values from -6 to 6
- prompt_len: int32 [2], replicated, may hold values from 4096 to 8192, as said below
- group_of: int32 [2], replicated, may hold values from 0 to 1, each once
- hidden: bfloat16 [4, 2, 8192], P(None, None, 'seq'), may hold values from -6 to 6
- norm_gain: float32 [8192], P('seq'), may hold values from 0.5 to 2
- w_qkv: bfloat16 [8192, 8, 768], P('seq', 'tp'), may hold values from -0.23204774 to 0.23204774
- w_out: bfloat16 [8, 512, 8192], P('tp', None, 'seq'), may hold values from -0.09375 to 0.09375
Outputs:
- attn_prefill: bfloat16 [2, 8192, 8, 512], P(None, 'seq', 'tp')
- cache_pages: bfloat16 [16384, 8, 256], P('seq', 'tp')
- decoded: bfloat16 [4, 2, 8192], P(None, None, 'seq')
Inputs may be any that keep to these rules, and one draw needn't show every extreme that they name: `prompt_len`: one prompt of every draw is 8192 long.
All inputs are finite; a program needn't handle non-finite values.
Results may differ from a plain program's by a relative error of at most 0.01.
Values may be sent and summed in bfloat16 or wider, within the bound.
A program may use at most 64 MiB of HBM per device.

v0:
```python
import math

import jax
import jax.numpy as jnp
from jax import lax
from jax.sharding import PartitionSpec as P

D = 8192


neg_big = -1e30
norm_eps = 1e-05
rope_base = 500000.0


def merged(shard, axis, combine):
    everything = jax.tree.map(lambda part: lax.all_gather(part, axis), shard)
    leading = jax.tree.map(lambda part: part[0], everything)

    def step(k, so_far):
        return combine(so_far, jax.tree.map(lambda part: part[k], everything))

    return lax.fori_loop(1, lax.axis_size(axis), step, leading)


def rotate(vectors, position):
    half_size = vectors.shape[-1] // 2
    frequency = rope_base ** (-2.0 * jnp.arange(half_size, dtype=jnp.float32) / vectors.shape[-1])
    angle = position * frequency
    cosine_wave = jnp.cos(angle)
    sine_wave = jnp.sin(angle)
    front_half = vectors[..., :half_size]
    back_half = vectors[..., half_size:]
    return jnp.concatenate(
        [
            front_half * cosine_wave - back_half * sine_wave,
            back_half * cosine_wave + front_half * sine_wave,
        ],
        axis=-1,
    )


def combine_parts(earlier, later):
    new_top = jnp.maximum(earlier[0], later[0])
    earlier_scale = jnp.exp(earlier[0] - new_top)
    later_scale = jnp.exp(later[0] - new_top)
    return (
        new_top,
        earlier[1] * earlier_scale + later[1] * later_scale,
        earlier[2] * earlier_scale[..., None] + later[2] * later_scale[..., None],
    )


def on_device(q_prefill, kv_prefill, prompt_len, group_of, hidden, norm_gain, w_qkv, w_out):
    cycle_size = lax.axis_size("seq")
    my_index = lax.axis_index("seq")
    n_prompts, row_count, kv_dev, q_width = q_prefill.shape
    head_size = kv_prefill.shape[-1] // 2
    per_kv = q_width // head_size
    group_size = cycle_size // n_prompts
    piece_rows = row_count // group_size
    score_scale = 1.0 / math.sqrt(head_size)
    row_pos = my_index * row_count + jnp.arange(row_count, dtype=jnp.int32)
    queries = q_prefill.reshape(n_prompts, row_count, kv_dev, per_kv, head_size)
    prompt_ids = jnp.arange(n_prompts, dtype=jnp.int32)
    my_group = my_index // group_size
    my_slot = my_index % group_size
    state_shape = (n_prompts, row_count, kv_dev, per_kv)
    empty_state = (
        jnp.full(state_shape, neg_big, jnp.float32),
        jnp.zeros(state_shape, jnp.float32),
        jnp.zeros(state_shape + (head_size,), jnp.float32),
    )
    start_state = (empty_state, jnp.zeros((1,), jnp.bfloat16))
    running = start_state[0]
    shard_piece = lax.all_gather(kv_prefill, "seq", axis=1, tiled=True)
    key_count = shard_piece.shape[1]
    block_rows = math.gcd(key_count, 1024)
    block_total = key_count // block_rows
    blocks = jnp.moveaxis(
        shard_piece.reshape(n_prompts, block_total, block_rows, kv_dev, 2 * head_size), 1, 0
    )

    def key_step(carried, block_item):
        row_top, row_total, weighted = carried
        key_block, block_position_index = block_item
        key_pos = block_position_index * block_rows + jnp.arange(block_rows, dtype=jnp.int32)
        allowed = (key_pos[None, None, :] <= row_pos[None, :, None]) & (
            key_pos[None, None, :] < prompt_len[:, None, None]
        )
        allowed = allowed[:, :, None, None, :]
        scores = (
            jnp.einsum(
                "prhqd,pnhd->prhqn",
                queries,
                key_block[..., :head_size],
                preferred_element_type=jnp.float32,
            )
            * score_scale
        )
        scores = jnp.where(allowed, scores, neg_big)
        new_top = jnp.maximum(row_top, jnp.max(scores, axis=-1))
        weight_matrices = jnp.exp(scores - new_top[..., None]) * allowed
        shrink = jnp.exp(row_top - new_top)
        row_total = row_total * shrink + jnp.sum(weight_matrices, axis=-1)
        weighted = weighted * shrink[..., None] + jnp.einsum(
            "prhqn,pnhd->prhqd",
            weight_matrices.astype(jnp.bfloat16),
            key_block[..., head_size:],
            preferred_element_type=jnp.float32,
        )
        return ((new_top, row_total, weighted), None)

    running, _ = lax.scan(key_step, running, (blocks, jnp.arange(block_total, dtype=jnp.int32)))
    row_top, row_total, weighted = running
    attn_prefill = (
        (weighted / row_total[..., None])
        .astype(jnp.bfloat16)
        .reshape(n_prompts, row_count, kv_dev, q_width)
    )
    prompt_of_group = jnp.sum(
        jnp.where(group_of[None, :] == prompt_ids[:, None], prompt_ids[None, :], 0), axis=1
    )
    chosen = jnp.take(kv_prefill, prompt_of_group, axis=0)
    outgoing = chosen.reshape(n_prompts * group_size, piece_rows, kv_dev, 2 * head_size)
    cache_pages = lax.all_to_all(outgoing, "seq", split_axis=0, concat_axis=0, tiled=True)
    page_rows = cache_pages.reshape(cycle_size * piece_rows, kv_dev, 2 * head_size)
    page_pos = (
        jnp.arange(cycle_size, dtype=jnp.int32)[:, None] * row_count
        + my_slot * piece_rows
        + jnp.arange(piece_rows, dtype=jnp.int32)[None, :]
    ).reshape(-1)
    page_allowed = (group_of == my_group)[:, None] & (page_pos[None, :] < prompt_len[:, None])
    page_allowed = page_allowed[:, None, None, :]
    page_value_rows = page_rows[..., head_size:].astype(jnp.float32)
    fresh_keys = []
    fresh_values = []
    outputs = []
    for step_index in range(hidden.shape[0]):
        current = hidden[step_index].astype(jnp.float32)
        squares = jnp.sum(current * current, axis=-1)
        scaled_in = (current * norm_gain).astype(jnp.bfloat16)
        partial_proj = jnp.einsum(
            "pe,ehw->phw", scaled_in, w_qkv, preferred_element_type=jnp.float32
        )
        squares, partial_proj = lax.psum((squares, partial_proj), "seq")
        projected = partial_proj * lax.rsqrt(squares / D + norm_eps)[:, None, None]
        position = (prompt_len + step_index).astype(jnp.float32)
        query_new = rotate(
            projected[..., :q_width].reshape(n_prompts, kv_dev, per_kv, head_size),
            position[:, None, None, None],
        ).astype(jnp.bfloat16)
        key_new = rotate(
            projected[..., q_width : q_width + head_size], position[:, None, None]
        ).astype(jnp.bfloat16)
        incoming_value = projected[..., q_width + head_size :].astype(jnp.bfloat16)
        fresh_keys.append(key_new)
        fresh_values.append(incoming_value)
        scores = (
            jnp.einsum(
                "nfae,rfe->nfar",
                query_new,
                page_rows[..., :head_size],
                preferred_element_type=jnp.float32,
            )
            * score_scale
        )
        scores = jnp.where(page_allowed, scores, neg_big)
        local_top = jnp.max(scores, axis=-1)
        weight_matrices = jnp.exp(scores - local_top[..., None]) * page_allowed
        local_total = jnp.sum(weight_matrices, axis=-1)
        local_weighted_values = jnp.einsum("oyjr,ryt->oyjt", weight_matrices, page_value_rows)
        cache_top, cache_total, cache_weighted = merged(
            (local_top, local_total, local_weighted_values), "seq", combine_parts
        )
        recent_keys = jnp.stack(fresh_keys, 0)
        recent_values = jnp.stack(fresh_values, 0).astype(jnp.float32)
        recent_scores = (
            jnp.einsum(
                "phqd,sphd->phqs", query_new, recent_keys, preferred_element_type=jnp.float32
            )
            * score_scale
        )
        best_top = jnp.maximum(cache_top, jnp.max(recent_scores, axis=-1))
        old_scale = jnp.exp(cache_top - best_top)
        recent_weights = jnp.exp(recent_scores - best_top[..., None])
        full_total = cache_total * old_scale + jnp.sum(recent_weights, axis=-1)
        full_weighted = cache_weighted * old_scale[..., None] + jnp.einsum(
            "phqs,sphd->phqd", recent_weights, recent_values
        )
        attended_new = (
            (full_weighted / full_total[..., None])
            .astype(jnp.bfloat16)
            .reshape(n_prompts, kv_dev, q_width)
        )
        partial_out = jnp.einsum(
            "phw,hwe->pe", attended_new, w_out, preferred_element_type=jnp.float32
        )
        head_mixed = lax.psum(partial_out, "tp")
        outputs.append((current + head_mixed).astype(jnp.bfloat16))
    return (attn_prefill, page_rows, jnp.stack(outputs, 0))


def solution(mesh):
    placed = (
        P(None, "seq", "tp", None),
        P(None, "seq", "tp", None),
        P(),
        P(),
        P(None, None, "seq"),
        P("seq"),
        P("seq", "tp", None),
        P("tp", None, "seq"),
    )
    return jax.shard_map(
        on_device,
        mesh=mesh,
        in_specs=placed,
        out_specs=(P(None, "seq", "tp", None), P("seq", "tp", None), P(None, None, "seq")),
        check_vma=False,
    )
```

profile of v0, /device:TPU:64, one launch (start us, length us, event | category | flops | bytes accessed | tf_op | source)
XLA Modules:
  0.0 848.3 jit_solution(4648860440604591879)
XLA Ops:
  8.9 1.5 gather_fusion
  11.2 8.3 all-to-all-start
  24.8 107.0 %all-reduce = (f32[2,1,768]{2,0,1:T(2,128)S(1)}, f32[2]{0:T(128)S(1)}, f32[2,1,768]{2,0,1:T(2,128)S(1)}, f32[2]{0:T(128)S(1)}, f32[2,1,768]{2,0,1:T(2,128)S(1)},...) all-reduce(f32[2,1,768]{2,0,1:T(2,128)S(1)} %convolution_bitcast_fu, ...), channel_id=1, replica_groups=mesh['seq'=32,'tp'=8] {'seq'}, use_global_device_ids=true, to_apply=%region_33.34 | all-reduce | flops 6152 | bytes 49216 | tf_op jit(solution)/shard_map/psum | solution.py:146
  139.0 55.9 %all-gather.18 = f32[32,2,4]{2,1,0:T(2,128)S(1)} all-gather(f32[1,2,4]{2,1,0:T(2,128)S(1)} %bitcast.736), channel_id=11, replica_groups=mesh['seq'=32,'tp'=8] {'seq'}, dimensions={0}, use_global_device_ids=true | all-gather | bytes 1056 | tf_op jit(solution)/shard_map/all_gather | solution.py:17
  194.9 41.4 %all-gather.19 = f32[32,2,4]{2,1,0:T(2,128)S(1)} all-gather(f32[1,2,4]{2,1,0:T(2,128)S(1)} %bitcast.737), channel_id=12, replica_groups=mesh['seq'=32,'tp'=8] {'seq'}, dimensions={0}, use_global_device_ids=true | all-gather | bytes 1056 | tf_op jit(solution)/shard_map/all_gather | solution.py:17
  236.3 37.9 %all-gather.11 = f32[64,1,4,128]{3,2,1,0:T(4,128)S(1)} all-gather(f32[2,1,4,128]{3,2,1,0:T(4,128)S(1)} %convolution_bitcast_fusion.5), channel_id=13, replica_groups=mesh['seq'=32,'tp'=8] {'seq'}, dimensions={0}, use_global_device_ids=true | all-gather | bytes 135168 | tf_op jit(solution)/shard_map/all_gather | solution.py:17
  274.2 3.7 while.94
  278.0 39.5 %all-gather.16 = f32[32,2,4]{2,1,0:T(2,128)S(1)} all-gather(f32[1,2,4]{2,1,0:T(2,128)S(1)} %bitcast.734), channel_id=8, replica_groups=mesh['seq'=32,'tp'=8] {'seq'}, dimensions={0}, use_global_device_ids=true | all-gather | bytes 1056 | tf_op jit(solution)/shard_map/all_gather | solution.py:17
  317.5 37.9 %all-gather.17 = f32[32,2,4]{2,1,0:T(2,128)S(1)} all-gather(f32[1,2,4]{2,1,0:T(2,128)S(1)} %bitcast.735), channel_id=9, replica_groups=mesh['seq'=32,'tp'=8] {'seq'}, dimensions={0}, use_global_device_ids=true | all-gather | bytes 1056 | tf_op jit(solution)/shard_map/all_gather | solution.py:17
  355.4 39.6 %all-gather.8 = f32[64,1,4,128]{3,2,1,0:T(4,128)S(1)} all-gather(f32[2,1,4,128]{3,2,1,0:T(4,128)S(1)} %convolution_bitcast_fusion.7), channel_id=10, replica_groups=mesh['seq'=32,'tp'=8] {'seq'}, dimensions={0}, use_global_device_ids=true | all-gather | bytes 135168 | tf_op jit(solution)/shard_map/all_gather | solution.py:17
  394.9 3.7 while.93
  398.7 37.9 %all-gather.14 = f32[32,2,4]{2,1,0:T(2,128)S(1)} all-gather(f32[1,2,4]{2,1,0:T(2,128)S(1)} %bitcast.732), channel_id=5, replica_groups=mesh['seq'=32,'tp'=8] {'seq'}, dimensions={0}, use_global_device_ids=true | all-gather | bytes 1056 | tf_op jit(solution)/shard_map/all_gather | solution.py:17
  436.6 39.3 %all-gather.15 = f32[32,2,4]{2,1,0:T(2,128)S(1)} all-gather(f32[1,2,4]{2,1,0:T(2,128)S(1)} %bitcast.733), channel_id=6, replica_groups=mesh['seq'=32,'tp'=8] {'seq'}, dimensions={0}, use_global_device_ids=true | all-gather | bytes 1056 | tf_op jit(solution)/shard_map/all_gather | solution.py:17
  475.8 38.2 %all-gather.5 = f32[64,1,4,128]{3,2,1,0:T(4,128)S(1)} all-gather(f32[2,1,4,128]{3,2,1,0:T(4,128)S(1)} %convolution_bitcast_fusion.8), channel_id=7, replica_groups=mesh['seq'=32,'tp'=8] {'seq'}, dimensions={0}, use_global_device_ids=true | all-gather | bytes 135168 | tf_op jit(solution)/shard_map/all_gather | solution.py:17
  514.1 3.7 while.92
  517.8 39.2 %all-gather.12 = f32[32,2,4]{2,1,0:T(2,128)S(1)} all-gather(f32[1,2,4]{2,1,0:T(2,128)S(1)} %bitcast.730), channel_id=2, replica_groups=mesh['seq'=32,'tp'=8] {'seq'}, dimensions={0}, use_global_device_ids=true | all-gather | bytes 1056 | tf_op jit(solution)/shard_map/all_gather | solution.py:17
  557.0 37.9 %all-gather.13 = f32[32,2,4]{2,1,0:T(2,128)S(1)} all-gather(f32[1,2,4]{2,1,0:T(2,128)S(1)} %bitcast.731), channel_id=3, replica_groups=mesh['seq'=32,'tp'=8] {'seq'}, dimensions={0}, use_global_device_ids=true | all-gather | bytes 1056 | tf_op jit(solution)/shard_map/all_gather | solution.py:17
  594.9 39.5 %all-gather.2 = f32[64,1,4,128]{3,2,1,0:T(4,128)S(1)} all-gather(f32[2,1,4,128]{3,2,1,0:T(4,128)S(1)} %convolution_bitcast_fusion.9), channel_id=4, replica_groups=mesh['seq'=32,'tp'=8] {'seq'}, dimensions={0}, use_global_device_ids=true | all-gather | bytes 135168 | tf_op jit(solution)/shard_map/all_gather | solution.py:17
  634.6 3.8 while.91
  639.7 30.9 %all-reduce.1 = (f32[2,256]{1,0:T(2,128)S(1)}, f32[2,256]{1,0:T(2,128)S(1)}, f32[2,256]{1,0:T(2,128)S(1)}, f32[2,256]{1,0:T(2,128)S(1)}) all-reduce(f32[2,256]{1,0:T(2,128)S(1)} %fusion.65, f32[2,256]{1,0:T(2,128)S(1)} %fusion.67, f32[2,256]{1,0:T(2,128)S(1)} %fusion.69, ...), channel_id=1, replica_groups=mesh['seq'=32,'tp'=8] {'tp'}, use_global_device_ids=true, to_apply=%region_42.43 | all-reduce | flops 2048 | bytes 16384 | tf_op jit(solution)/shard_map/psum | solution.py:199
  671.7 165.7 %while.95 = (s32[]{:T(128)}, f32[2,256,1,4]{1,3,0,2:T(4,128)S(1)}, f32[2,256,1,4]{1,3,0,2:T(4,128)}, f32[2,256,1,4,128]{1,4,3,0,2:T(8,128)}, s32[8]{0:T(128)}, /...) while((s32[]{:T(128)}, f32[2,256,1,4]{1,3,0,2:T(4,128)S(1)}, ...), condition=%wide.region_3.4_spmd.clone, body=%wide.region_0.3_spmd.clone.sunk | while | flops 1103117568 | bytes 82004288 | solution.py:114
  674.9 1.3 dynamic-slice_bitcast_fusion.2
  677.2 4.7 fusion.291
  682.0 5.2 fusion.293
  688.0 3.5 fusion.294
  697.1 4.7 fusion.291
  701.8 5.2 fusion.293
  707.8 4.6 fusion.294
  717.9 4.7 fusion.291
  722.6 5.2 fusion.293
  728.7 4.6 fusion.294
  738.7 4.7 fusion.291
  743.5 5.2 fusion.293
  749.5 4.6 fusion.294
  759.6 4.7 fusion.291
  764.3 5.2 fusion.293
  770.4 4.6 fusion.294
  780.4 4.7 fusion.291
  785.1 5.2 fusion.293
  791.2 4.6 fusion.294
  801.3 4.7 fusion.291
  806.0 5.2 fusion.293
  812.0 4.6 fusion.294
  822.1 4.7 fusion.291
  826.8 5.2 fusion.293
  832.9 4.6 fusion.294
  837.4 1.3 divide_convert_fusion
  839.8 1.7 copy.263
  (774 shorter events, 76.4 us)
Async XLA Ops:
  7.2 13.3 %copy-start = (bf16[256,1,768]{2,0,1:T(8,128)(2,1)S(1)}, bf16[256,1,768]{2,0,1:T(8,128)(2,1)}, u32[]{:S(2)}) copy-start(bf16[256,1,768]{2,0,1:T(8,128)(2,1)} %param.24) | copy-start | bytes 1179652
  7.2 663.4 %copy-start.8 = (bf16[4,2,256]{2,1,0:T(2,128)(2,1)S(1)}, bf16[4,2,256]{2,1,0:T(2,128)(2,1)}, u32[]{:S(2)}) copy-start(bf16[4,2,256]{2,1,0:T(2,128)(2,1)} %param.22) | copy-start | bytes 12292
  7.2 631.9 %copy-start.4 = (bf16[1,512,256]{2,1,0:T(8,128)(2,1)S(1)}, bf16[1,512,256]{2,1,0:T(8,128)(2,1)}, u32[]{:S(2)}) copy-start(bf16[1,512,256]{2,1,0:T(8,128)(2,1)} %param.25) | copy-start | bytes 786436
  7.2 664.0 %all-gather.22.cloned.1.call-start = ((), (), s32[]{:S(2)}) async-start(), calls=%async_computation.1 | async-start | bytes 8650752 | tf_op jit(solution)/shard_map/all_gather | solution.py:76
  11.2 125.7 %all-to-all-start = ((bf16[32,16,1,256]{3,1,2,0:T(8,128)(2,1)}), bf16[32,16,1,256]{3,1,2,0:T(8,128)(2,1)S(1)}, u32[]{:S(2)}, u32[]{:S(2)}) async-start(bf16[32,16,1,256]{3,1,2,0:T(8,128)(2,1)} %broadcast_select_fusion), calls=%async_computation | async-start | bytes 524288 | tf_op jit(solution)/shard_map/all_to_all | solution.py:126
  136.9 534.8 %copy-start.5 = (bf16[32,16,1,256]{3,1,2,0:T(8,128)(2,1)}, bf16[32,16,1,256]{3,1,2,0:T(8,128)(2,1)S(1)}, u32[]{:S(2)}) copy-start(bf16[32,16,1,256]{3,1,2,0:T(8,128)(2,1)S(1)} %all-to-all-done) | copy-start | bytes 786436
  676.2 1.0 copy-start.2
  681.9 5.3 copy-start.6
  681.9 5.8 copy-start.1
  681.9 6.1 copy-start.3
  687.2 4.3 copy-start.7
  696.0 1.0 copy-start.2
  701.7 5.3 copy-start.6
  701.7 5.8 copy-start.1
  701.7 6.1 copy-start.3
  707.0 5.3 copy-start.7
  716.9 1.0 copy-start.2
  722.6 5.3 copy-start.6
  722.6 5.8 copy-start.1
  722.6 6.1 copy-start.3
  727.9 5.3 copy-start.7
  737.7 1.0 copy-start.2
  743.4 5.3 copy-start.6
  743.4 5.8 copy-start.1
  743.4 6.1 copy-start.3
  748.7 5.3 copy-start.7
  758.5 1.0 copy-start.2
  764.3 5.3 copy-start.6
  764.3 5.8 copy-start.1
  764.3 6.1 copy-start.3
  769.6 5.3 copy-start.7
  779.4 1.0 copy-start.2
  785.1 5.3 copy-start.6
  785.1 5.8 copy-start.1
  785.1 6.1 copy-start.3
  790.4 5.3 copy-start.7
  800.2 1.0 copy-start.2
  806.0 5.3 copy-start.6
  806.0 5.8 copy-start.1
  806.0 6.1 copy-start.3
  811.3 5.3 copy-start.7
  821.1 1.0 copy-start.2
  826.8 5.3 copy-start.6
  826.8 5.8 copy-start.1
  826.8 6.1 copy-start.3
  832.1 5.3 copy-start.7
Sparse Core Ops, SparseCore 0:
  9.9 70.9 all-gather.21
where the time goes:
time: 862 us; the launch traced here: 848 us
  blocking collectives  622 us (72%)
  matrix products  80.3 us (9%)
  other arithmetic  74.2 us (9%)
  local copies, waits for them, and re-layouts  41.7 us (5%)
  between operations  14.4 us (2%)
    all_gather x12, blocking collectives, merged(): everything = jax.tree.map(lambda part: lax.all_gather(part, axis), shard)  484 us
    psum x1, blocking collectives, on_device(): squares, partial_proj = lax.psum((squares, partial_proj), 'seq')  107 us
    reduce_sum x8, other arithmetic, key_step(): row_total = row_total * shrink + jnp.sum(weight_matrices, axis=-1)  41.8 us
    dot_general x8, matrix products, key_step(): jnp.einsum('prhqd,pnhd->prhqn', queries, key_block[..., :head_size], pref...  37.5 us
    dot_general x8, matrix products, key_step(): jnp.einsum('prhqn,pnhd->prhqd', weight_matrices.astype(jnp.bfloat16), key...  35.4 us
    psum x1, blocking collectives, on_device(): head_mixed = lax.psum(partial_out, 'tp')  30.9 us
  transfers between devices with their start and end apart: 2, of which 0 were waited for; matrix products, arithmetic and copies ran while one was open for 4% of the time, Pallas kernels for 0%

commit v1 on v0

v1 whole, which is shorter than its diff:
```python
import functools
import math

import jax
import jax.numpy as jnp
from jax import lax
from jax.experimental import pallas as pl
from jax.experimental.pallas import tpu as pltpu
from jax.sharding import PartitionSpec as P

MESH = pl.DeviceIdType.MESH
NEG = -1e30
EPS = 1e-05
BASE = 500000.0
ROWS = 256
BLOCK = 512
HD = 128
HEADS = 4
PART_A = 128
PART_B = BLOCK - PART_A
HALF_A, HALF_B = PART_A // 2, PART_B // 2
NY = 4
NZ = 4
NX = 4
BF16 = jnp.bfloat16
F32 = jnp.float32
NT = (((1,), (1,)), ((), ()))


def kernel(
    width,
    lens_ref, q_ref, kv_ref, hid_ref, gain_ref, wqkv_ref, wout_ref, cos_ref, sin_ref,
    attn_ref, dec_ref,
    blocks, q_in, q_scaled, acc, tops, o_in, o_out,
    proj_core, proj_y, proj_z, soft_y, soft_z, att_core, out_x, out_h,
    swap_send, swap_recv,
    zb_send, zb_recv, za_send, za_recv,
    yb_send, yb_recv, yf_send, ya_send, ya_recv, yaf_send,
    peer_send, pc_recv, py_recv, pz_recv, sy_recv, sz_recv, ac_recv, ox_recv, oh_recv,
):
    seq = lax.axis_index("seq")
    tp = lax.axis_index("tp")
    z, y, k = seq // 8, (seq // 2) % NY, seq % 2
    x, zh = tp // 2, tp % 2
    chip = seq // 2
    other = 1 - k

    def at(dz=0, dy=0, core=None):
        return {
            "seq": (z + dz) * 8 + lax.rem(y + dy, NY) * 2 + (k if core is None else core),
            "tp": tp,
        }

    partner = at(core=other)
    up, down = at(dy=1), at(dy=3)

    def y_peer(d):
        return at(dy=d)

    def z_peer(d):
        return {"seq": lax.rem(z + d, NZ) * 8 + y * 2 + k, "tp": tp}

    def x_peer(d):
        return {"seq": seq, "tp": lax.rem(x + d, NX) * 2 + zh}

    h_peer = {"seq": seq, "tp": x * 2 + 1 - zh}

    def copy(src, dst, ssem, rsem, dev):
        return pltpu.make_async_remote_copy(
            src_ref=src, dst_ref=dst, send_sem=ssem, recv_sem=rsem, device_id=dev, device_id_type=MESH
        )

    barrier = pltpu.get_barrier_semaphore()
    peers = [partner, h_peer]
    for d in (1, 2, 3):
        peers += [y_peer(d), z_peer(d), x_peer(d)]
    for dev in peers:
        pl.semaphore_signal(barrier, inc=1, device_id=dev, device_id_type=MESH)
    pl.semaphore_wait(barrier, len(peers))

    swap_kv = copy(
        kv_ref.at[other],
        blocks.at[z, y, pl.ds(pl.multiple_of(k * ROWS, ROWS), ROWS)],
        swap_send.at[0], swap_recv.at[0], partner,
    )
    swap_q = copy(q_ref.at[other], q_in, swap_send.at[1], swap_recv.at[1], partner)
    swap_kv.start()
    swap_q.start()
    blocks[z, y, pl.ds(pl.multiple_of(k * ROWS, ROWS), ROWS), :] = kv_ref[k]

    hid = hid_ref[...].astype(F32)
    squares = jnp.sum(hid * hid, axis=-1, keepdims=True)
    scaled_in = (hid * gain_ref[...]).astype(BF16)
    part = jnp.dot(scaled_in, wqkv_ref[...], preferred_element_type=F32)
    proj_core[k] = jnp.concatenate([part, jnp.broadcast_to(squares, (8, HD))], axis=1)
    core_send = copy(proj_core.at[k], proj_core.at[k], peer_send.at[0], pc_recv.at[k], partner)
    core_send.start()

    def spread(buf, peer, mine, n_peers, sends, first, recv):
        for d in range(1, n_peers + 1):
            copy(buf.at[mine], buf.at[mine], sends.at[first + d - 1], recv.at[mine], peer(d)).start()

    def gathered(buf, peer, mine, n_peers, sends, first, recv):
        for d in range(1, n_peers + 1):
            src = lax.rem(mine + d, n_peers + 1)
            c = copy(buf.at[src], buf.at[src], sends.at[first + d - 1], recv.at[src], peer(d))
            c.wait()

    def scale_queries(ref_rows, r):
        c = math.log2(math.e) / math.sqrt(HD)
        for h in range(HEADS):
            wide = ref_rows(h).astype(F32) * c
            top = wide.astype(BF16)
            q_scaled[2 * h + r] = jnp.concatenate([top, (wide - top.astype(F32)).astype(BF16)], axis=1)

    scale_queries(lambda h: q_ref[k, :, h * HD : (h + 1) * HD], 0)
    acc[...] = jnp.zeros_like(acc)
    tops[...] = jnp.full_like(tops, NEG)
    length = lens_ref[k]

    def attend(load, n, key_pos, causal):
        ones = jnp.ones((n, HD), BF16)
        bias = jnp.where(key_pos < length, 0.0, NEG)
        if causal:
            shape = (ROWS, n)
            row = lax.broadcasted_iota(jnp.int32, shape, 0)
            col = lax.broadcasted_iota(jnp.int32, shape, 1)

        @pl.loop(0, HEADS)
        def _(h):
            keys, values = load()
            keys = jnp.concatenate([keys, keys], axis=1)
            values = jnp.concatenate([values, ones], axis=1)
            for r in (0, 1):
                i = 2 * h + r
                s = lax.dot_general(q_scaled[i], keys, NT, preferred_element_type=F32)
                if causal:
                    s = jnp.where(col <= row + (k if r == 0 else other) * ROWS, s + bias, NEG)
                else:
                    s = s + bias
                before = tops[i]
                now = jnp.maximum(before, jnp.max(s, axis=-1, keepdims=True))
                p = jnp.exp2(s - jnp.concatenate([now] * (n // HD), axis=1))
                shrink = jnp.exp2(before - now)
                o = jnp.dot(p.astype(BF16), values, preferred_element_type=F32)
                acc[i] = acc[i] * jnp.concatenate([shrink, shrink], axis=1) + o
                tops[i] = now

    def positions(n):
        return lax.broadcasted_iota(jnp.int32, (1, n), 1)

    def whole_block(yp):
        def load():
            return blocks[z, yp, :, 0:HD], blocks[z, yp, :, HD : 2 * HD]

        return load

    def part_b(zp, yp):
        def load():
            at_b = blocks.at[zp, yp]
            return at_b[PART_A:BLOCK, 0:HD], at_b[PART_A:BLOCK, HD : 2 * HD]

        attend(load, PART_B, (zp * NY + yp) * BLOCK + PART_A + positions(PART_B), False)

    def part_a(zp):
        def load():
            rows = [blocks[zp, yp, 0:PART_A, :] for yp in range(NY)]
            rows = jnp.concatenate(rows, axis=0)
            return rows[:, 0:HD], rows[:, HD : 2 * HD]

        pos = positions(NY * PART_A)
        attend(load, NY * PART_A, zp * NY * BLOCK + (pos // PART_A) * BLOCK + pos % PART_A, False)

    a_rows = pl.ds(0, PART_A)
    b_rows = pl.ds(PART_A, PART_B)
    a_half = [pl.ds(0, HALF_A), pl.ds(HALF_A, HALF_A)]
    b_half = [pl.ds(PART_A, HALF_B), pl.ds(PART_A + HALF_B, HALF_B)]

    def moved(zp, yp, rows, ssem, rsem, dev):
        return copy(blocks.at[zp, yp, rows], blocks.at[zp, yp, rows], ssem, rsem, dev)

    def zb(zp):
        return moved(zp, y, b_rows, zb_send.at[zp], zb_recv.at[zp], z_peer(1))

    def za(zp, yp):
        return moved(zp, yp, a_rows, za_send.at[zp, yp], za_recv.at[zp, yp], z_peer(1))

    def yb(zp, direction, half, yp=None):
        return moved(
            zp, y if yp is None else yp, b_half[half],
            yb_send.at[zp, direction, half], yb_recv.at[zp, direction, half], (up, down)[direction],
        )

    def yb_forward(zp, direction):
        yp = lax.rem(y + (3, 1)[direction], NY)
        return moved(
            zp, yp, b_half[direction],
            yf_send.at[zp, direction], yb_recv.at[zp, 2, direction], (up, down)[direction],
        )

    def ya(direction, half, yp=None):
        return moved(
            z, y if yp is None else yp, a_half[half],
            ya_send.at[direction, half], ya_recv.at[direction, half], (up, down)[direction],
        )

    def ya_forward(direction):
        yp = lax.rem(y + (3, 1)[direction], NY)
        return moved(
            z, yp, a_half[direction],
            yaf_send.at[direction], ya_recv.at[2, direction], (up, down)[direction],
        )

    y_minus, y_plus, y_far = lax.rem(y + 3, NY), lax.rem(y + 1, NY), lax.rem(y + 2, NY)

    def send_b(zp):
        @pl.when(z < NZ - 1)
        def _():
            zb(zp).start()

        yb(zp, 0, 0).start()
        yb(zp, 1, 1).start()
        yb(zp, 0, 1).start()
        yb(zp, 1, 0).start()

    def forward_b(zp):
        yb(zp, 0, 0, y_minus).wait_recv()
        yb_forward(zp, 0).start()
        yb(zp, 1, 1, y_plus).wait_recv()
        yb_forward(zp, 1).start()

    def far_b(zp):
        for half in (0, 1):
            moved(zp, y_far, b_half[half], yf_send.at[zp, half], yb_recv.at[zp, 2, half], up).wait_recv()

    copy(
        kv_ref.at[k],
        blocks.at[z, y, pl.ds(pl.multiple_of(other * ROWS, ROWS), ROWS)],
        swap_send.at[0], swap_recv.at[0], partner,
    ).wait_recv()
    send_b(z)
    for half in (0, 1):
        ya(0, half).start()
        ya(1, 1 - half).start()

    @pl.when(z < NZ - 1)
    def _():
        za(z, y).start()

    copy(proj_core.at[other], proj_core.at[other], peer_send.at[0], pc_recv.at[other], partner).wait()
    proj_y[y] = proj_core[0] + proj_core[1]
    spread(proj_y, y_peer, y, 3, peer_send, 1, py_recv)

    swap_q.wait_recv()
    scale_queries(lambda h: q_in[:, h * HD : (h + 1) * HD], 1)
    attend(whole_block(y), BLOCK, chip * BLOCK + positions(BLOCK), True)

    gathered(proj_y, y_peer, y, 3, peer_send, 1, py_recv)
    proj_z[z] = (proj_y[0] + proj_y[1]) + (proj_y[2] + proj_y[3])
    spread(proj_z, z_peer, z, 3, peer_send, 4, pz_recv)

    forward_b(z)
    ya(0, 0, y_minus).wait_recv()
    ya_forward(0).start()
    ya(1, 1, y_plus).wait_recv()
    ya_forward(1).start()
    ya(0, 1, y_minus).wait_recv()
    ya(1, 0, y_plus).wait_recv()

    def next_b(j):
        @pl.when(j <= z)
        def _():
            zb(z - j).wait_recv()
            send_b(z - j)

    @pl.when(z < NZ - 1)
    def _():
        za(z, y_minus).start()
        za(z, y_plus).start()

    next_b(1)
    yb(z, 0, 1, y_minus).wait_recv()
    yb(z, 1, 0, y_plus).wait_recv()
    for half in (0, 1):
        moved(z, y_far, a_half[half], yaf_send.at[half], ya_recv.at[2, half], up).wait_recv()

    @pl.when(z < NZ - 1)
    def _():
        za(z, y_far).start()

    gathered(proj_z, z_peer, z, 3, peer_send, 4, pz_recv)
    total = (proj_z[0] + proj_z[1]) + (proj_z[2] + proj_z[3])
    proj = total[:, : 6 * HD] * lax.rsqrt(total[:, 6 * HD :][:, :1] / width + EPS)
    cosine, sine = cos_ref[...], sin_ref[...]

    def rotated(v):
        return (v * cosine + pltpu.roll(v, HD // 2, 1) * sine).astype(BF16)

    queries = jnp.concatenate([rotated(proj[:, h * HD : (h + 1) * HD]) for h in range(HEADS)], axis=0)
    blank = jnp.zeros((HD - 8, HD), F32)
    new_key = jnp.concatenate([rotated(proj[:, 4 * HD : 5 * HD]).astype(F32), blank], axis=0).astype(BF16)
    new_value = jnp.concatenate([proj[:, 5 * HD : 6 * HD], blank], axis=0).astype(BF16)
    own = blocks[z, y]
    keys = jnp.concatenate([own[:, :HD], new_key], axis=0)
    values = jnp.concatenate([own[:, HD:], new_value], axis=0)
    s = lax.dot_general(queries, keys, NT, preferred_element_type=F32) * (1.0 / math.sqrt(HD))
    row = lax.broadcasted_iota(jnp.int32, s.shape, 0) % 8
    col = lax.broadcasted_iota(jnp.int32, s.shape, 1)
    new = col - BLOCK
    old_ok = (col < BLOCK) & (chip * BLOCK + col < length)
    new_ok = (new >= 0) & (new <= row) & (new % 2 == row % 2) & (chip == 0)
    s = jnp.where(old_ok | new_ok, s, NEG)
    top = jnp.max(s, axis=-1, keepdims=True)
    p = jnp.exp(s - top)
    soft_y[y, 0] = jnp.dot(p.astype(BF16), values, preferred_element_type=F32)
    lane = lax.broadcasted_iota(jnp.int32, (32, HD), 1)

    def packed(top, sums):
        return jnp.where(lane < HD // 2, top, sums)

    soft_y[y, 1] = packed(top, jnp.sum(p, axis=-1, keepdims=True))
    spread(soft_y, y_peer, y, 3, peer_send, 7, sy_recv)

    def merge(buf):
        m = [buf[i, 1][:, :1] for i in range(4)]
        l = [buf[i, 1][:, HD - 1 :] for i in range(4)]
        top = jnp.maximum(jnp.maximum(m[0], m[1]), jnp.maximum(m[2], m[3]))
        w = [jnp.exp(t - top) for t in m]
        sums = (l[0] * w[0] + l[1] * w[1]) + (l[2] * w[2] + l[3] * w[3])
        o = (buf[0, 0] * w[0] + buf[1, 0] * w[1]) + (buf[2, 0] * w[2] + buf[3, 0] * w[3])
        return top, sums, o

    def decode_1():
        gathered(soft_y, y_peer, y, 3, peer_send, 7, sy_recv)
        top, sums, o = merge(soft_y)
        soft_z[z, 0] = o
        soft_z[z, 1] = packed(top, sums)
        spread(soft_z, z_peer, z, 3, peer_send, 10, sz_recv)

    def decode_2():
        gathered(soft_z, z_peer, z, 3, peer_send, 10, sz_recv)
        _, sums, o = merge(soft_z)
        att_core[k] = (o / sums).astype(BF16)
        copy(att_core.at[k], att_core.at[k], peer_send.at[13], ac_recv.at[k], partner).start()

    def decode_3():
        copy(att_core.at[other], att_core.at[other], peer_send.at[13], ac_recv.at[other], partner).wait()
        of_first = lax.broadcasted_iota(jnp.int32, (32, HD), 0) % 2 == 0
        att = jnp.where(of_first, att_core[0].astype(F32), att_core[1].astype(F32))
        out = jnp.zeros((8, ROWS), F32)
        for h in range(HEADS):
            out += jnp.dot(
                att[8 * h : 8 * h + 8].astype(BF16), wout_ref[h * HD : (h + 1) * HD, :],
                preferred_element_type=F32,
            )
        out_x[x] = out
        spread(out_x, x_peer, x, 3, peer_send, 14, ox_recv)

    def decode_4():
        gathered(out_x, x_peer, x, 3, peer_send, 14, ox_recv)
        out_h[zh] = (out_x[0] + out_x[1]) + (out_x[2] + out_x[3])
        copy(out_h.at[zh], out_h.at[zh], peer_send.at[17], oh_recv.at[zh], h_peer).start()

    def decode_5():
        copy(out_h.at[1 - zh], out_h.at[1 - zh], peer_send.at[17], oh_recv.at[1 - zh], h_peer).wait()
        dec_ref[...] = (hid_ref[...].astype(F32) + (out_h[0] + out_h[1])).astype(BF16)

    @pl.loop(1, 4)
    def _(d):
        yp = lax.rem(y + jnp.where(d == 1, 3, jnp.where(d == 2, 1, 2)), NY)

        @pl.when(d == 3)
        def _():
            far_b(z)

        @pl.when(yp < y)
        def _():
            attend(whole_block(yp), BLOCK, (z * NY + yp) * BLOCK + positions(BLOCK), False)

    decode_1()

    @pl.loop(1, NZ)
    def _(j):
        @pl.when(j <= z)
        def _():
            zp = z - j
            part_b(zp, y)
            forward_b(zp)
            next_b(j + 1)

            @pl.loop(1, 4)
            def _(d):
                yp = lax.rem(y + jnp.where(d == 1, 3, jnp.where(d == 2, 1, 2)), NY)

                @pl.when(d == 1)
                def _():
                    yb(zp, 0, 1, y_minus).wait_recv()

                @pl.when(d == 2)
                def _():
                    yb(zp, 1, 0, y_plus).wait_recv()

                @pl.when(d == 3)
                def _():
                    far_b(zp)

                part_b(zp, yp)

            for yp in range(NY):
                za(zp, yp).wait_recv()

            @pl.when(z < NZ - 1)
            def _():
                for yp in range(NY):
                    za(zp, yp).start()

            part_a(zp)

        @pl.when(j == 1)
        def _():
            decode_2()

        @pl.when(j == 2)
        def _():
            decode_3()

        @pl.when(j == 3)
        def _():
            decode_4()

    def result(i):
        return (acc[i][:, :HD] / acc[i][:, HD:]).astype(BF16)

    for h in range(HEADS):
        o_out[:, h * HD : (h + 1) * HD] = result(2 * h + 1)
    back = copy(o_out, o_in, swap_send.at[2], swap_recv.at[2], partner)
    back.start()
    for h in range(HEADS):
        attn_ref[k, :, h * HD : (h + 1) * HD] = result(2 * h)
    decode_5()

    swap_kv.wait_send()
    swap_q.wait_send()

    @pl.when(z < NZ - 1)
    def _():
        @pl.loop(0, NZ)
        def _(zp):
            @pl.when(zp <= z)
            def _():
                zb(zp).wait_send()
                for yp in range(NY):
                    za(zp, yp).wait_send()

    @pl.loop(0, NZ)
    def _(zp):
        @pl.when(zp <= z)
        def _():
            for direction in (0, 1):
                for half in (0, 1):
                    yb(zp, direction, half).wait_send()
                yb_forward(zp, direction).wait_send()

    for direction in (0, 1):
        for half in (0, 1):
            ya(direction, half).wait_send()
        ya_forward(direction).wait_send()
    back.wait()
    attn_ref[other] = o_in[...]


def on_device(q_prefill, kv_prefill, prompt_len, group_of, hidden, norm_gain, w_qkv, w_out):
    n_prompts, rows = q_prefill.shape[:2]
    cycle = lax.axis_size("seq")
    group_size = cycle // n_prompts
    piece = rows // group_size
    prompt_ids = jnp.arange(n_prompts, dtype=jnp.int32)
    prompt_of_group = jnp.sum(
        jnp.where(group_of[None, :] == prompt_ids[:, None], prompt_ids[None, :], 0), axis=1
    )
    chosen = jnp.take(kv_prefill, prompt_of_group, axis=0)
    outgoing = chosen.reshape(n_prompts * group_size, piece, 1, 2 * HD)
    cache_pages = lax.all_to_all(outgoing, "seq", split_axis=0, concat_axis=0, tiled=True)
    cache_pages = cache_pages.reshape(cycle * piece, 1, 2 * HD)

    steps = hidden.shape[0]
    half = HD // 2
    frequency = BASE ** (-2.0 * jnp.arange(half, dtype=F32) / HD)
    position = (prompt_len[None, :] + jnp.arange(steps, dtype=jnp.int32)[:, None]).reshape(-1)
    angle = position.astype(F32)[:, None] * frequency
    cosine, sine = jnp.cos(angle), jnp.sin(angle)
    cosine = jnp.concatenate([cosine, cosine], axis=1)
    sine = jnp.concatenate([-sine, sine], axis=1)

    vmem = pl.BlockSpec(memory_space=pltpu.VMEM)
    dma = pltpu.SemaphoreType.DMA
    width = hidden.shape[2] * cycle
    attn, decoded = pl.pallas_call(
        functools.partial(kernel, float(width)),
        out_shape=(
            jax.ShapeDtypeStruct((n_prompts, rows, HEADS * HD), BF16),
            jax.ShapeDtypeStruct((steps * n_prompts, rows), BF16),
        ),
        in_specs=[pl.BlockSpec(memory_space=pltpu.SMEM)] + [vmem] * 8,
        out_specs=(vmem, vmem),
        scratch_shapes=[
            pltpu.VMEM((NZ, NY, BLOCK, 2 * HD), BF16),
            pltpu.VMEM((ROWS, HEADS * HD), BF16),
            pltpu.VMEM((2 * HEADS, ROWS, 2 * HD), BF16),
            pltpu.VMEM((2 * HEADS, ROWS, 2 * HD), F32),
            pltpu.VMEM((2 * HEADS, ROWS, HD), F32),
            pltpu.VMEM((ROWS, HEADS * HD), BF16),
            pltpu.VMEM((ROWS, HEADS * HD), BF16),
            pltpu.VMEM((2, 8, 7 * HD), F32),
            pltpu.VMEM((NY, 8, 7 * HD), F32),
            pltpu.VMEM((NZ, 8, 7 * HD), F32),
            pltpu.VMEM((NY, 2, 32, HD), F32),
            pltpu.VMEM((NZ, 2, 32, HD), F32),
            pltpu.VMEM((2, 32, HD), BF16),
            pltpu.VMEM((NX, 8, ROWS), F32),
            pltpu.VMEM((2, 8, ROWS), F32),
            dma((3,)), dma((3,)),
            dma((NZ,)), dma((NZ,)), dma((NZ, NY)), dma((NZ, NY)),
            dma((NZ, 2, 2)), dma((NZ, 3, 2)), dma((NZ, 2)), dma((2, 2)), dma((3, 2)), dma((2,)),
            dma((18,)), dma((2,)), dma((NY,)), dma((NZ,)), dma((NY,)), dma((NZ,)), dma((2,)), dma((NX,)), dma((2,)),
        ],
        compiler_params=pltpu.CompilerParams(
            collective_id=0, has_side_effects=True, vmem_limit_bytes=40 * 1024 * 1024
        ),
        cost_estimate=pl.CostEstimate(flops=9 * 10**9, bytes_accessed=3 * 10**6, transcendentals=17 * 10**6),
    )(
        prompt_len,
        q_prefill.reshape(n_prompts, rows, HEADS * HD),
        kv_prefill.reshape(n_prompts, rows, 2 * HD),
        hidden.reshape(steps * n_prompts, rows),
        norm_gain.reshape(1, rows),
        w_qkv.reshape(rows, 6 * HD),
        w_out.reshape(HEADS * HD, rows),
        cosine,
        sine,
    )
    return (
        attn.reshape(n_prompts, rows, 1, HEADS * HD),
        cache_pages,
        decoded.reshape(steps, n_prompts, rows),
    )


def solution(mesh):
    placed = (
        P(None, "seq", "tp", None),
        P(None, "seq", "tp", None),
        P(),
        P(),
        P(None, None, "seq"),
        P("seq"),
        P("seq", "tp", None),
        P("tp", None, "seq"),
    )
    return jax.shard_map(
        on_device,
        mesh=mesh,
        in_specs=placed,
        out_specs=(P(None, "seq", "tp", None), P("seq", "tp", None), P(None, None, "seq")),
        check_vma=False,
    )
```

time: 862 us -> 96.8 us (0.11)
  the two profiles are of different devices: /device:TPU:64 before, /device:TPU:96 now
where the time goes in v1:
time: 96.8 us; the launch traced here: 96.6 us
  Pallas kernels  80.8 us (83%)
  starting transfers between devices  8.06 us (8%)
  local copies, waits for them, and re-layouts  5.22 us (5%)
  other arithmetic  1.8 us (2%)
    pallas_call x1, Pallas kernels, on_device(): pl.pallas_call(functools.partial(kernel, float(width)), out_shape=(jax.Sh...  80.8 us
    all_to_all x1, starting transfers between devices, on_device(): lax.all_to_all(outgoing, 'seq', split_axis=0, concat_axis=0, tiled=True)  8.06 us
    unnamed x16, local copies, waits for them, and re-layouts  2.8 us
  transfers between devices with their start and end apart: 1, of which 0 were waited for; matrix products, arithmetic and copies ran while one was open for 1% of the time, Pallas kernels for 84%

profile of v1, /device:TPU:96, one launch (start us, length us, event | category | flops | bytes accessed | tf_op | source)
XLA Modules:
  0.0 96.6 jit_solution(2549101582445664152)
XLA Ops:
  0.6 0.8 fusion
  1.4 0.1 broadcast_in_dim.35
  1.5 0.1 broadcast_in_dim.36
  1.6 0.0 copy-start.3
  1.6 1.6 %gather_fusion = bf16[2,256,256]{2,1,0:T(8,128)(2,1)S(1)} fusion(bf16[2,256,256]{2,1,0:T(8,128)(2,1)} %bitcast.17, s32[1024]{0:T(1024)S(1)} %pad_clamp_fusion), kind=kCustom, calls=%fused_computation | custom fusion | bytes 524296 | tf_op jit(solution)/shard_map/jit(_take)/gather | solution.py:481
  3.2 0.0 copy-start.2
  3.2 0.8 broadcast_select_fusion
  4.0 0.0 copy-start
  4.0 0.0 copy-start.4
  4.0 8.1 %all-to-all-start = ((bf16[32,16,1,256]{3,1,2,0:T(8,128)(2,1)}), bf16[32,16,1,256]{3,1,2,0:T(8,128)(2,1)S(1)}, u32[]{:S(2)}, u32[]{:S(2)}) async-start(bf16[32,16,1,256]{3,1,2,0:T(8,128)(2,1)} %broadcast_select_fusion), calls=%async_computation | async-start | bytes 524288 | tf_op jit(solution)/shard_map/all_to_all | solution.py:483
  12.1 0.0 copy-start.1
  12.1 0.0 copy-start.6
  12.1 0.6 copy-done.1
  12.7 0.1 convert_element_type.11
  12.8 0.0 copy-done.6
  12.8 0.1 fusion.1
  12.9 0.1 pad_maximum_fusion
  13.0 0.0 copy-start.5
  13.0 0.0 copy-done.3
  13.0 0.0 copy-done.2
  13.0 0.0 copy-done
  13.0 0.0 copy-done.4
  13.1 0.7 copy-done.5
  13.7 80.8 %shard_map.103 = (bf16[2,256,512]{2,1,0:T(8,128)(2,1)S(1)}, bf16[8,256]{1,0:T(8,128)(2,1)S(1)}) custom-call(s32[2]{0:T(128)S(1)} %copy-done.1, bf16[2,256,512]{2,1,0:T(8,128)(2,1)S(1)} %bitcast.19, bf16[2,256,256]{2,1,0:T(8,128)(2,1)S(1)} %bitcast.18, bf16[8,256]{1,0:T(8,128)(2,1)S(1)} %reshape.89.hid_ref, f32[1,256]{1,0:T(1,128)S(1)} %bitcast.22, ...), custom_call_target="tpu_custom_call" | custom-call | flops 8999999488 | bytes 3000000 | tf_op jit(solution)/shard_map/pallas_call | solution.py:498
  94.5 0.6 reshape.95
  95.1 0.0 all-to-all-done
  95.1 0.8 copy.19
  95.9 0.7 copy.20
  (6 shorter events, 0.0 us)
Async XLA Ops:
  1.6 11.4 %copy-start.3 = (bf16[256,1,768]{2,0,1:T(8,128)(2,1)S(1)}, bf16[256,1,768]{2,0,1:T(8,128)(2,1)}, u32[]{:S(2)}) copy-start(bf16[256,1,768]{2,0,1:T(8,128)(2,1)} %param.14) | copy-start | bytes 1179652
  3.2 9.9 %copy-start.2 = (bf16[2,256,1,512]{3,1,2,0:T(8,128)(2,1)S(1)}, bf16[2,256,1,512]{3,1,2,0:T(8,128)(2,1)}, u32[]{:S(2)}) copy-start(bf16[2,256,1,512]{3,1,2,0:T(8,128)(2,1)} %param.8) | copy-start | bytes 1572868
  4.0 9.0 %copy-start = (bf16[2,256,1,256]{3,1,2,0:T(8,128)(2,1)S(1)}, bf16[2,256,1,256]{3,1,2,0:T(8,128)(2,1)}, u32[]{:S(2)}) copy-start(bf16[2,256,1,256]{3,1,2,0:T(8,128)(2,1)} %param.9) | copy-start | bytes 786436
  4.0 9.1 %copy-start.4 = (bf16[1,512,256]{2,1,0:T(8,128)(2,1)S(1)}, bf16[1,512,256]{2,1,0:T(8,128)(2,1)}, u32[]{:S(2)}) copy-start(bf16[1,512,256]{2,1,0:T(8,128)(2,1)} %param.15) | copy-start | bytes 786436
  4.0 91.1 %all-to-all-start = ((bf16[32,16,1,256]{3,1,2,0:T(8,128)(2,1)}), bf16[32,16,1,256]{3,1,2,0:T(8,128)(2,1)S(1)}, u32[]{:S(2)}, u32[]{:S(2)}) async-start(bf16[32,16,1,256]{3,1,2,0:T(8,128)(2,1)} %broadcast_select_fusion), calls=%async_computation | async-start | bytes 524288 | tf_op jit(solution)/shard_map/all_to_all | solution.py:483
  12.1 0.7 copy-start.1
  12.1 0.7 copy-start.6
  13.0 0.7 copy-start.5

commit v2 on v1

--- a/solution.py
+++ b/solution.py
@@ -20,6 +20,8 @@
 PART_B = BLOCK - PART_A
 HALF_A, HALF_B = PART_A // 2, PART_B // 2
 NY = 4
+N_SEQ = 32
+PIECE = 16
 NZ = 4
 NX = 4
 BF16 = jnp.bfloat16
@@ -29,14 +31,15 @@
 
 def kernel(
     width,
-    lens_ref, q_ref, kv_ref, hid_ref, gain_ref, wqkv_ref, wout_ref, cos_ref, sin_ref,
-    attn_ref, dec_ref,
+    lens_ref, group_ref, q_ref, kv_ref, hid_ref, gain_ref, wqkv_ref, wout_ref, cos_ref, sin_ref,
+    attn_ref, pages_ref, dec_ref,
     blocks, q_in, q_scaled, acc, tops, o_in, o_out,
-    proj_core, proj_y, proj_z, soft_y, soft_z, att_core, out_x, out_h,
+    proj_core, proj_y, proj_z, soft_y, soft_z, att_core, out_x, out_h, by_group, pages,
     swap_send, swap_recv,
     zb_send, zb_recv, za_send, za_recv,
     yb_send, yb_recv, yf_send, ya_send, ya_recv, yaf_send,
     peer_send, pc_recv, py_recv, pz_recv, sy_recv, sz_recv, ac_recv, ox_recv, oh_recv,
+    page_send, page_recv, page_own,
 ):
     seq = lax.axis_index("seq")
     tp = lax.axis_index("tp")
@@ -71,12 +74,34 @@
         )
 
     barrier = pltpu.get_barrier_semaphore()
-    peers = [partner, h_peer]
-    for d in (1, 2, 3):
-        peers += [y_peer(d), z_peer(d), x_peer(d)]
+    peers = [h_peer, x_peer(1), x_peer(2), x_peer(3)]
     for dev in peers:
         pl.semaphore_signal(barrier, inc=1, device_id=dev, device_id_type=MESH)
-    pl.semaphore_wait(barrier, len(peers))
+
+    @pl.loop(1, N_SEQ)
+    def _(d):
+        dev = {"seq": lax.rem(seq + d, N_SEQ), "tp": tp}
+        pl.semaphore_signal(barrier, inc=1, device_id=dev, device_id_type=MESH)
+
+    second = (group_ref[0] != 0).astype(jnp.int32)
+    by_group[0] = kv_ref[second].reshape(N_SEQ // 2, PIECE, 2 * HD)
+    by_group[1] = kv_ref[1 - second].reshape(N_SEQ // 2, PIECE, 2 * HD)
+
+    def page(owner, source):
+        dev = {"seq": owner, "tp": tp}
+        return copy(
+            by_group.at[owner // 16, lax.rem(owner, 16)], pages.at[source],
+            page_send.at[owner], page_recv.at[source], dev,
+        )
+
+    hid = hid_ref[...].astype(F32)
+    squares = jnp.sum(hid * hid, axis=-1, keepdims=True)
+    scaled_in = (hid * gain_ref[...]).astype(BF16)
+    part = jnp.dot(scaled_in, wqkv_ref[...], preferred_element_type=F32)
+    proj_core[k] = jnp.concatenate([part, jnp.broadcast_to(squares, (8, HD))], axis=1)
+    blocks[z, y, pl.ds(pl.multiple_of(k * ROWS, ROWS), ROWS), :] = kv_ref[k]
+
+    pl.semaphore_wait(barrier, len(peers) + N_SEQ - 1)
 
     swap_kv = copy(
         kv_ref.at[other],
@@ -86,15 +111,15 @@
     swap_q = copy(q_ref.at[other], q_in, swap_send.at[1], swap_recv.at[1], partner)
     swap_kv.start()
     swap_q.start()
-    blocks[z, y, pl.ds(pl.multiple_of(k * ROWS, ROWS), ROWS), :] = kv_ref[k]
-
-    hid = hid_ref[...].astype(F32)
-    squares = jnp.sum(hid * hid, axis=-1, keepdims=True)
-    scaled_in = (hid * gain_ref[...]).astype(BF16)
-    part = jnp.dot(scaled_in, wqkv_ref[...], preferred_element_type=F32)
-    proj_core[k] = jnp.concatenate([part, jnp.broadcast_to(squares, (8, HD))], axis=1)
     core_send = copy(proj_core.at[k], proj_core.at[k], peer_send.at[0], pc_recv.at[k], partner)
     core_send.start()
+
+    @pl.loop(1, N_SEQ)
+    def _(d):
+        page(lax.rem(seq + d, N_SEQ), seq).start()
+
+    own_page = pltpu.make_async_copy(by_group.at[seq // 16, lax.rem(seq, 16)], pages.at[seq], page_own)
+    own_page.start()
 
     def spread(buf, peer, mine, n_peers, sends, first, recv):
         for d in range(1, n_peers + 1):
@@ -118,58 +143,47 @@
     tops[...] = jnp.full_like(tops, NEG)
     length = lens_ref[k]
 
-    def attend(load, n, key_pos, causal):
-        ones = jnp.ones((n, HD), BF16)
+    def attend(keys, values, key_pos, causal=False):
+        n = keys.shape[0]
         bias = jnp.where(key_pos < length, 0.0, NEG)
+        keys = jnp.concatenate([keys, keys], axis=1)
+        values = jnp.concatenate([values, jnp.ones((n, HD), BF16)], axis=1)
         if causal:
-            shape = (ROWS, n)
-            row = lax.broadcasted_iota(jnp.int32, shape, 0)
-            col = lax.broadcasted_iota(jnp.int32, shape, 1)
-
-        @pl.loop(0, HEADS)
-        def _(h):
-            keys, values = load()
-            keys = jnp.concatenate([keys, keys], axis=1)
-            values = jnp.concatenate([values, ones], axis=1)
-            for r in (0, 1):
-                i = 2 * h + r
-                s = lax.dot_general(q_scaled[i], keys, NT, preferred_element_type=F32)
-                if causal:
-                    s = jnp.where(col <= row + (k if r == 0 else other) * ROWS, s + bias, NEG)
-                else:
-                    s = s + bias
-                before = tops[i]
-                now = jnp.maximum(before, jnp.max(s, axis=-1, keepdims=True))
-                p = jnp.exp2(s - jnp.concatenate([now] * (n // HD), axis=1))
-                shrink = jnp.exp2(before - now)
-                o = jnp.dot(p.astype(BF16), values, preferred_element_type=F32)
-                acc[i] = acc[i] * jnp.concatenate([shrink, shrink], axis=1) + o
-                tops[i] = now
+            row = lax.broadcasted_iota(jnp.int32, (ROWS, n), 0)
+            col = lax.broadcasted_iota(jnp.int32, (ROWS, n), 1)
+            seen = [jnp.where(col <= row + core * ROWS, bias, NEG) for core in (k, other)]
+
+        def scores(i):
+            s = lax.dot_general(q_scaled[i], keys, NT, preferred_element_type=F32)
+            return s + (seen[i % 2] if causal else bias)
+
+        s = scores(0)
+        for i in range(2 * HEADS):
+            ahead = scores(i + 1) if i + 1 < 2 * HEADS else None
+            before = tops[i]
+            now = jnp.maximum(before, jnp.max(s, axis=-1, keepdims=True))
+            p = jnp.exp2(s - jnp.concatenate([now] * (n // HD), axis=1)).astype(BF16)
+            shrink = jnp.exp2(before - now)
+            tops[i] = now
+            o = jnp.dot(p, values, preferred_element_type=F32)
+            acc[i] = acc[i] * jnp.concatenate([shrink, shrink], axis=1) + o
+            s = ahead
 
     def positions(n):
         return lax.broadcasted_iota(jnp.int32, (1, n), 1)
 
-    def whole_block(yp):
-        def load():
-            return blocks[z, yp, :, 0:HD], blocks[z, yp, :, HD : 2 * HD]
-
-        return load
-
-    def part_b(zp, yp):
-        def load():
-            at_b = blocks.at[zp, yp]
-            return at_b[PART_A:BLOCK, 0:HD], at_b[PART_A:BLOCK, HD : 2 * HD]
-
-        attend(load, PART_B, (zp * NY + yp) * BLOCK + PART_A + positions(PART_B), False)
-
-    def part_a(zp):
-        def load():
-            rows = [blocks[zp, yp, 0:PART_A, :] for yp in range(NY)]
-            rows = jnp.concatenate(rows, axis=0)
-            return rows[:, 0:HD], rows[:, HD : 2 * HD]
-
-        pos = positions(NY * PART_A)
-        attend(load, NY * PART_A, zp * NY * BLOCK + (pos // PART_A) * BLOCK + pos % PART_A, False)
+    def whole_block(yp, causal=False):
+        rows = blocks[z, yp]
+        attend(rows[:, :HD], rows[:, HD:], (z * NY + yp) * BLOCK + positions(BLOCK), causal)
+
+    def parts(zp, in_b, with_a):
+        rows = [blocks[zp, yp, PART_A:BLOCK, :] for yp in in_b]
+        pos = [(zp * NY + yp) * BLOCK + PART_A + positions(PART_B) for yp in in_b]
+        if with_a:
+            rows += [blocks[zp, yp, 0:PART_A, :] for yp in range(NY)]
+            pos += [(zp * NY + yp) * BLOCK + positions(PART_A) for yp in range(NY)]
+        rows = jnp.concatenate(rows, axis=0)
+        attend(rows[:, :HD], rows[:, HD:], jnp.concatenate(pos, axis=1))
 
     a_rows = pl.ds(0, PART_A)
     b_rows = pl.ds(PART_A, PART_B)
@@ -253,11 +267,7 @@
 
     swap_q.wait_recv()
     scale_queries(lambda h: q_in[:, h * HD : (h + 1) * HD], 1)
-    attend(whole_block(y), BLOCK, chip * BLOCK + positions(BLOCK), True)
-
-    gathered(proj_y, y_peer, y, 3, peer_send, 1, py_recv)
-    proj_z[z] = (proj_y[0] + proj_y[1]) + (proj_y[2] + proj_y[3])
-    spread(proj_z, z_peer, z, 3, peer_send, 4, pz_recv)
+    whole_block(y, True)
 
     forward_b(z)
     ya(0, 0, y_minus).wait_recv()
@@ -288,38 +298,44 @@
     def _():
         za(z, y_far).start()
 
-    gathered(proj_z, z_peer, z, 3, peer_send, 4, pz_recv)
-    total = (proj_z[0] + proj_z[1]) + (proj_z[2] + proj_z[3])
-    proj = total[:, : 6 * HD] * lax.rsqrt(total[:, 6 * HD :][:, :1] / width + EPS)
-    cosine, sine = cos_ref[...], sin_ref[...]
-
-    def rotated(v):
-        return (v * cosine + pltpu.roll(v, HD // 2, 1) * sine).astype(BF16)
-
-    queries = jnp.concatenate([rotated(proj[:, h * HD : (h + 1) * HD]) for h in range(HEADS)], axis=0)
-    blank = jnp.zeros((HD - 8, HD), F32)
-    new_key = jnp.concatenate([rotated(proj[:, 4 * HD : 5 * HD]).astype(F32), blank], axis=0).astype(BF16)
-    new_value = jnp.concatenate([proj[:, 5 * HD : 6 * HD], blank], axis=0).astype(BF16)
-    own = blocks[z, y]
-    keys = jnp.concatenate([own[:, :HD], new_key], axis=0)
-    values = jnp.concatenate([own[:, HD:], new_value], axis=0)
-    s = lax.dot_general(queries, keys, NT, preferred_element_type=F32) * (1.0 / math.sqrt(HD))
-    row = lax.broadcasted_iota(jnp.int32, s.shape, 0) % 8
-    col = lax.broadcasted_iota(jnp.int32, s.shape, 1)
-    new = col - BLOCK
-    old_ok = (col < BLOCK) & (chip * BLOCK + col < length)
-    new_ok = (new >= 0) & (new <= row) & (new % 2 == row % 2) & (chip == 0)
-    s = jnp.where(old_ok | new_ok, s, NEG)
-    top = jnp.max(s, axis=-1, keepdims=True)
-    p = jnp.exp(s - top)
-    soft_y[y, 0] = jnp.dot(p.astype(BF16), values, preferred_element_type=F32)
     lane = lax.broadcasted_iota(jnp.int32, (32, HD), 1)
 
     def packed(top, sums):
         return jnp.where(lane < HD // 2, top, sums)
 
-    soft_y[y, 1] = packed(top, jnp.sum(p, axis=-1, keepdims=True))
-    spread(soft_y, y_peer, y, 3, peer_send, 7, sy_recv)
+    def decode_0():
+        gathered(proj_y, y_peer, y, 3, peer_send, 1, py_recv)
+        proj_z[z] = (proj_y[0] + proj_y[1]) + (proj_y[2] + proj_y[3])
+        spread(proj_z, z_peer, z, 3, peer_send, 4, pz_recv)
+
+    def decode_1():
+        gathered(proj_z, z_peer, z, 3, peer_send, 4, pz_recv)
+        total = (proj_z[0] + proj_z[1]) + (proj_z[2] + proj_z[3])
+        proj = total[:, : 6 * HD] * lax.rsqrt(total[:, 6 * HD :][:, :1] / width + EPS)
+        cosine, sine = cos_ref[...], sin_ref[...]
+
+        def rotated(v):
+            return (v * cosine + pltpu.roll(v, HD // 2, 1) * sine).astype(BF16)
+
+        queries = jnp.concatenate([rotated(proj[:, h * HD : (h + 1) * HD]) for h in range(HEADS)], axis=0)
+        blank = jnp.zeros((HD - 8, HD), F32)
+        new_key = jnp.concatenate([rotated(proj[:, 4 * HD : 5 * HD]).astype(F32), blank], axis=0).astype(BF16)
+        new_value = jnp.concatenate([proj[:, 5 * HD : 6 * HD], blank], axis=0).astype(BF16)
+        own = blocks[z, y]
+        keys = jnp.concatenate([own[:, :HD], new_key], axis=0)
+        values = jnp.concatenate([own[:, HD:], new_value], axis=0)
+        s = lax.dot_general(queries, keys, NT, preferred_element_type=F32) * (1.0 / math.sqrt(HD))
+        row = lax.broadcasted_iota(jnp.int32, s.shape, 0) % 8
+        col = lax.broadcasted_iota(jnp.int32, s.shape, 1)
+        new = col - BLOCK
+        old_ok = (col < BLOCK) & (chip * BLOCK + col < length)
+        new_ok = (new >= 0) & (new <= row) & (new % 2 == row % 2) & (chip == 0)
+        s = jnp.where(old_ok | new_ok, s, NEG)
+        top = jnp.max(s, axis=-1, keepdims=True)
+        p = jnp.exp(s - top)
+        soft_y[y, 0] = jnp.dot(p.astype(BF16), values, preferred_element_type=F32)
+        soft_y[y, 1] = packed(top, jnp.sum(p, axis=-1, keepdims=True))
+        spread(soft_y, y_peer, y, 3, peer_send, 7, sy_recv)
 
     def merge(buf):
         m = [buf[i, 1][:, :1] for i in range(4)]
@@ -330,20 +346,20 @@
         o = (buf[0, 0] * w[0] + buf[1, 0] * w[1]) + (buf[2, 0] * w[2] + buf[3, 0] * w[3])
         return top, sums, o
 
-    def decode_1():
+    def decode_2():
         gathered(soft_y, y_peer, y, 3, peer_send, 7, sy_recv)
         top, sums, o = merge(soft_y)
         soft_z[z, 0] = o
         soft_z[z, 1] = packed(top, sums)
         spread(soft_z, z_peer, z, 3, peer_send, 10, sz_recv)
 
-    def decode_2():
+    def decode_3():
         gathered(soft_z, z_peer, z, 3, peer_send, 10, sz_recv)
         _, sums, o = merge(soft_z)
         att_core[k] = (o / sums).astype(BF16)
         copy(att_core.at[k], att_core.at[k], peer_send.at[13], ac_recv.at[k], partner).start()
 
-    def decode_3():
+    def decode_4():
         copy(att_core.at[other], att_core.at[other], peer_send.at[13], ac_recv.at[other], partner).wait()
         of_first = lax.broadcasted_iota(jnp.int32, (32, HD), 0) % 2 == 0
         att = jnp.where(of_first, att_core[0].astype(F32), att_core[1].astype(F32))
@@ -356,12 +372,12 @@
         out_x[x] = out
         spread(out_x, x_peer, x, 3, peer_send, 14, ox_recv)
 
-    def decode_4():
+    def decode_5():
         gathered(out_x, x_peer, x, 3, peer_send, 14, ox_recv)
         out_h[zh] = (out_x[0] + out_x[1]) + (out_x[2] + out_x[3])
         copy(out_h.at[zh], out_h.at[zh], peer_send.at[17], oh_recv.at[zh], h_peer).start()
 
-    def decode_5():
+    def decode_6():
         copy(out_h.at[1 - zh], out_h.at[1 - zh], peer_send.at[17], oh_recv.at[1 - zh], h_peer).wait()
         dec_ref[...] = (hid_ref[...].astype(F32) + (out_h[0] + out_h[1])).astype(BF16)
 
@@ -375,37 +391,44 @@
 
         @pl.when(yp < y)
         def _():
-            attend(whole_block(yp), BLOCK, (z * NY + yp) * BLOCK + positions(BLOCK), False)
-
-    decode_1()
+            whole_block(yp)
+
+        @pl.when(d == 1)
+        def _():
+            decode_0()
+
+        @pl.when(d == 3)
+        def _():
+            decode_1()
 
     @pl.loop(1, NZ)
     def _(j):
         @pl.when(j <= z)
         def _():
             zp = z - j
-            part_b(zp, y)
+            parts(zp, [y], False)
             forward_b(zp)
             next_b(j + 1)
 
-            @pl.loop(1, 4)
-            def _(d):
-                yp = lax.rem(y + jnp.where(d == 1, 3, jnp.where(d == 2, 1, 2)), NY)
-
-                @pl.when(d == 1)
-                def _():
-                    yb(zp, 0, 1, y_minus).wait_recv()
-
-                @pl.when(d == 2)
-                def _():
-                    yb(zp, 1, 0, y_plus).wait_recv()
-
-                @pl.when(d == 3)
-                def _():
-                    far_b(zp)
-
-                part_b(zp, yp)
-
+        @pl.when(j == 1)
+        def _():
+            decode_2()
+
+        @pl.when(j == 2)
+        def _():
+            decode_4()
+
+        @pl.when(j == 3)
+        def _():
+            decode_6()
+
+        @pl.when(j <= z)
+        def _():
+            zp = z - j
+            yb(zp, 0, 1, y_minus).wait_recv()
+            yb(zp, 1, 0, y_plus).wait_recv()
+            parts(zp, [y_minus, y_plus], False)
+            far_b(zp)
             for yp in range(NY):
                 za(zp, yp).wait_recv()
 
@@ -414,19 +437,15 @@
                 for yp in range(NY):
                     za(zp, yp).start()
 
-            part_a(zp)
+            parts(zp, [y_far], True)
 
         @pl.when(j == 1)
         def _():
-            decode_2()
+            decode_3()
 
         @pl.when(j == 2)
         def _():
-            decode_3()
-
-        @pl.when(j == 3)
-        def _():
-            decode_4()
+            decode_5()
 
     def result(i):
         return (acc[i][:, :HD] / acc[i][:, HD:]).astype(BF16)
@@ -437,10 +456,16 @@
     back.start()
     for h in range(HEADS):
         attn_ref[k, :, h * HD : (h + 1) * HD] = result(2 * h)
-    decode_5()
 
     swap_kv.wait_send()
     swap_q.wait_send()
+    own_page.wait()
+
+    @pl.loop(1, N_SEQ)
+    def _(d):
+        page(lax.rem(seq + d, N_SEQ), lax.rem(seq + d, N_SEQ)).wait()
+
+    pages_ref[...] = pages[...].reshape(N_SEQ * PIECE, 2 * HD)
 
     @pl.when(z < NZ - 1)
     def _():
@@ -472,16 +497,6 @@
 def on_device(q_prefill, kv_prefill, prompt_len, group_of, hidden, norm_gain, w_qkv, w_out):
     n_prompts, rows = q_prefill.shape[:2]
     cycle = lax.axis_size("seq")
-    group_size = cycle // n_prompts
-    piece = rows // group_size
-    prompt_ids = jnp.arange(n_prompts, dtype=jnp.int32)
-    prompt_of_group = jnp.sum(
-        jnp.where(group_of[None, :] == prompt_ids[:, None], prompt_ids[None, :], 0), axis=1
-    )
-    chosen = jnp.take(kv_prefill, prompt_of_group, axis=0)
-    outgoing = chosen.reshape(n_prompts * group_size, piece, 1, 2 * HD)
-    cache_pages = lax.all_to_all(outgoing, "seq", split_axis=0, concat_axis=0, tiled=True)
-    cache_pages = cache_pages.reshape(cycle * piece, 1, 2 * HD)
 
     steps = hidden.shape[0]
     half = HD // 2
@@ -495,14 +510,15 @@
     vmem = pl.BlockSpec(memory_space=pltpu.VMEM)
     dma = pltpu.SemaphoreType.DMA
     width = hidden.shape[2] * cycle
-    attn, decoded = pl.pallas_call(
+    attn, pages, decoded = pl.pallas_call(
         functools.partial(kernel, float(width)),
         out_shape=(
             jax.ShapeDtypeStruct((n_prompts, rows, HEADS * HD), BF16),
+            jax.ShapeDtypeStruct((N_SEQ * PIECE, 2 * HD), BF16),
             jax.ShapeDtypeStruct((steps * n_prompts, rows), BF16),
         ),
-        in_specs=[pl.BlockSpec(memory_space=pltpu.SMEM)] + [vmem] * 8,
-        out_specs=(vmem, vmem),
+        in_specs=[pl.BlockSpec(memory_space=pltpu.SMEM)] * 2 + [vmem] * 8,
+        out_specs=(vmem, vmem, vmem),
         scratch_shapes=[
             pltpu.VMEM((NZ, NY, BLOCK, 2 * HD), BF16),
             pltpu.VMEM((ROWS, HEADS * HD), BF16),
@@ -519,10 +535,13 @@
             pltpu.VMEM((2, 32, HD), BF16),
             pltpu.VMEM((NX, 8, ROWS), F32),
             pltpu.VMEM((2, 8, ROWS), F32),
+            pltpu.VMEM((2, N_SEQ // 2, PIECE, 2 * HD), BF16),
+            pltpu.VMEM((N_SEQ, PIECE, 2 * HD), BF16),
             dma((3,)), dma((3,)),
             dma((NZ,)), dma((NZ,)), dma((NZ, NY)), dma((NZ, NY)),
             dma((NZ, 2, 2)), dma((NZ, 3, 2)), dma((NZ, 2)), dma((2, 2)), dma((3, 2)), dma((2,)),
             dma((18,)), dma((2,)), dma((NY,)), dma((NZ,)), dma((NY,)), dma((NZ,)), dma((2,)), dma((NX,)), dma((2,)),
+            dma((N_SEQ,)), dma((N_SEQ,)), dma,
         ],
         compiler_params=pltpu.CompilerParams(
             collective_id=0, has_side_effects=True, vmem_limit_bytes=40 * 1024 * 1024
@@ -530,6 +549,7 @@
         cost_estimate=pl.CostEstimate(flops=9 * 10**9, bytes_accessed=3 * 10**6, transcendentals=17 * 10**6),
     )(
         prompt_len,
+        group_of,
         q_prefill.reshape(n_prompts, rows, HEADS * HD),
         kv_prefill.reshape(n_prompts, rows, 2 * HD),
         hidden.reshape(steps * n_prompts, rows),
@@ -541,7 +561,7 @@
     )
     return (
         attn.reshape(n_prompts, rows, 1, HEADS * HD),
-        cache_pages,
+        pages.reshape(N_SEQ * PIECE, 1, 2 * HD),
         decoded.reshape(steps, n_prompts, rows),
     )
 

time: 96.8 us -> 72.7 us (0.75)
  the two profiles are of different devices: /device:TPU:96 before, /device:TPU:97 now
where the time goes in v2:
time: 72.7 us; the launch traced here: 72.5 us
  Pallas kernels  64.2 us (88%)
  local copies, waits for them, and re-layouts  7.44 us (10%)
    pallas_call x1, Pallas kernels, on_device(): pl.pallas_call(functools.partial(kernel, float(width)), out_shape=(jax.Sh...  64.2 us
    unnamed x18, local copies, waits for them, and re-layouts  6.75 us

profile of v2, /device:TPU:97, one launch (start us, length us, event | category | flops | bytes accessed | tf_op | source)
XLA Modules:
  0.0 72.5 jit_solution(7063798003332686313)
XLA Ops:
  0.6 0.0 copy-start
  0.6 0.0 copy-start.7
  0.7 0.6 copy-done
  1.3 0.1 convert_element_type.11
  1.4 0.0 copy-done.7
  1.4 0.1 fusion
  1.5 0.1 pad_maximum_fusion
  1.6 0.0 copy-start.5
  1.6 0.0 copy-start.6
  1.6 0.7 copy-done.5
  2.3 0.0 copy-done.6
  2.3 0.0 copy-start.1
  2.3 1.0 %copy-done.1 = bf16[2,256,1,512]{3,1,2,0:T(8,128)(2,1)S(1)} copy-done((bf16[2,256,1,512]{3,1,2,0:T(8,128)(2,1)S(1)}, bf16[2,256,1,512]{3,1,2,0:T(8,128)(2,1)}, u32[]{:S(2)}) %copy-start.1) | copy-done | bytes 524312
  3.3 0.0 copy-start.2
  3.3 1.0 %copy-done.2 = bf16[256,1,768]{2,0,1:T(8,128)(2,1)S(1)} copy-done((bf16[256,1,768]{2,0,1:T(8,128)(2,1)S(1)}, bf16[256,1,768]{2,0,1:T(8,128)(2,1)}, u32[]{:S(2)}) %copy-start.2) | copy-done | bytes 393240
  4.3 0.0 copy-start.3
  4.3 0.9 %copy-done.3 = bf16[2,256,1,256]{3,1,2,0:T(8,128)(2,1)S(1)} copy-done((bf16[2,256,1,256]{3,1,2,0:T(8,128)(2,1)S(1)}, bf16[2,256,1,256]{3,1,2,0:T(8,128)(2,1)}, u32[]{:S(2)}) %copy-start.3) | copy-done | bytes 262168
  5.3 0.0 copy-start.4
  5.3 0.9 %copy-done.4 = bf16[1,512,256]{2,1,0:T(8,128)(2,1)S(1)} copy-done((bf16[1,512,256]{2,1,0:T(8,128)(2,1)S(1)}, bf16[1,512,256]{2,1,0:T(8,128)(2,1)}, u32[]{:S(2)}) %copy-start.4) | copy-done | bytes 262168
  6.2 64.2 %shard_map.103 = (bf16[2,256,512]{2,1,0:T(8,128)(2,1)S(1)}, bf16[512,256]{1,0:T(8,128)(2,1)S(1)}, bf16[8,256]{1,0:T(8,128)(2,1)S(1)}) custom-call(s32[2]{0:T(128)S(1)} %copy-done, s32[2]{0:T(128)S(1)} %copy-done.6, bf16[2,256,512]{2,1,0:T(8,128)(2,1)S(1)} %bitcast.11, bf16[2,256,256]{2,1,0:T(8,128)(2,1)S(1)} %bitcast.13, ...), custom_call_target="tpu_custom_call" | custom-call | flops 8999999488 | bytes 3000000 | tf_op jit(solution)/shard_map/pallas_call | solution.py:513
  70.4 0.6 reshape.62
  71.0 0.8 %copy.15 = bf16[2,256,1,512]{3,1,2,0:T(8,128)(2,1)} copy(bf16[2,256,1,512]{3,1,2,0:T(8,128)(2,1)S(1)} %bitcast.9) | data formatting | bytes 1048576
  71.8 0.7 copy.16
  (3 shorter events, 0.0 us)
Async XLA Ops:
  0.6 0.7 copy-start
  0.6 0.7 %copy-start.7 = (bf16[4,2,256]{2,1,0:T(2,128)(2,1)S(1)}, bf16[4,2,256]{2,1,0:T(2,128)(2,1)}, u32[]{:S(2)}) copy-start(bf16[4,2,256]{2,1,0:T(2,128)(2,1)} %param.12) | copy-start | bytes 12292
  1.6 0.7 copy-start.5
  1.6 0.7 copy-start.6
  2.3 1.0 %copy-start.1 = (bf16[2,256,1,512]{3,1,2,0:T(8,128)(2,1)S(1)}, bf16[2,256,1,512]{3,1,2,0:T(8,128)(2,1)}, u32[]{:S(2)}) copy-start(bf16[2,256,1,512]{3,1,2,0:T(8,128)(2,1)} %param.8) | copy-start | bytes 1572868
  3.3 1.0 %copy-start.2 = (bf16[256,1,768]{2,0,1:T(8,128)(2,1)S(1)}, bf16[256,1,768]{2,0,1:T(8,128)(2,1)}, u32[]{:S(2)}) copy-start(bf16[256,1,768]{2,0,1:T(8,128)(2,1)} %param.14) | copy-start | bytes 1179652
  4.3 0.9 %copy-start.3 = (bf16[2,256,1,256]{3,1,2,0:T(8,128)(2,1)S(1)}, bf16[2,256,1,256]{3,1,2,0:T(8,128)(2,1)}, u32[]{:S(2)}) copy-start(bf16[2,256,1,256]{3,1,2,0:T(8,128)(2,1)} %param.9) | copy-start | bytes 786436
  5.3 0.9 %copy-start.4 = (bf16[1,512,256]{2,1,0:T(8,128)(2,1)S(1)}, bf16[1,512,256]{2,1,0:T(8,128)(2,1)}, u32[]{:S(2)}) copy-start(bf16[1,512,256]{2,1,0:T(8,128)(2,1)} %param.15) | copy-start | bytes 786436

commit v3 on v0

v3 whole, which is shorter than its diff:
```python
import functools
import math

import jax
import jax.numpy as jnp
import numpy as np
from jax import lax
from jax.experimental import pallas as pl
from jax.experimental.pallas import tpu as pltpu
from jax.sharding import PartitionSpec as P

MESH = pl.DeviceIdType.MESH
NEG = -1e30
EPS = 1e-05
BASE = 500000.0
ROWS = 256
BLOCK = 512
HD = 128
HEADS = 4
NY = 4
NZ = 4
ROW = 8
N_TP = 8
EARLY = 1
N_SEQ = 32
PIECE = 16
BF16 = jnp.bfloat16
F32 = jnp.float32
NT = (((1,), (1,)), ((), ()))


def kernel(
    width,
    lens_ref, group_ref, q_ref, kv_ref, hid_ref, gain_ref, wqkv_ref, wout_ref, freq_ref,
    attn_ref, pages_ref, dec_ref,
    blocks, kv_own, q_own, q_in, wqkv, wout, q_scaled, acc, tops, o_in, o_out, o_own,
    proj_row, proj_z, soft_row, soft_z, out_tp, by_group, pages,
    local, swap_send, swap_recv, chunk_recv, chip_recv,
    first_send, forward_send, chip_send, far_send,
    peer_send, pr_recv, pz_recv, sr_recv, sz_recv, ot_recv,
    page_send, page_recv,
):
    seq = lax.axis_index("seq")
    tp = lax.axis_index("tp")
    z, y, k = seq // 8, (seq // 2) % NY, seq % 2
    big, s = z // 2, z % 2
    other = 1 - k

    def on(zz, yy, core):
        return {"seq": zz * 8 + yy * 2 + core, "tp": tp}

    mate = on(z, y, other)
    pair = on(big * 2 + 1 - s, y, k)
    up, down = on(z, lax.rem(y + 1, NY), k), on(z, lax.rem(y + 3, NY), k)

    def row_peer(d):
        place = lax.rem(2 * y + k + d, ROW)
        return on(z, place // 2, lax.rem(place, 2))

    def z_peer(d):
        return on(lax.rem(z + d, NZ), y, k)

    def tp_peer(d):
        return {"seq": seq, "tp": lax.rem(tp + d, N_TP)}

    def copy(src, dst, ssem, rsem, dev):
        return pltpu.make_async_remote_copy(
            src_ref=src, dst_ref=dst, send_sem=ssem, recv_sem=rsem, device_id=dev, device_id_type=MESH
        )

    loads = [
        pltpu.make_async_copy(src, dst, local.at[i])
        for i, (src, dst) in enumerate([
            (kv_ref, kv_own), (kv_ref.at[s], blocks.at[big, y, s, k]), (wqkv_ref, wqkv),
            (q_ref.at[s], q_own), (wout_ref, wout),
        ])
    ]
    for load in loads:
        load.start()

    barrier = pltpu.get_barrier_semaphore()

    @pl.loop(1, N_TP)
    def _(d):
        pl.semaphore_signal(barrier, inc=1, device_id=tp_peer(d), device_id_type=MESH)

    @pl.loop(1, N_SEQ)
    def _(d):
        dev = {"seq": lax.rem(seq + d, N_SEQ), "tp": tp}
        pl.semaphore_signal(barrier, inc=1, device_id=dev, device_id_type=MESH)

    acc[...] = jnp.zeros_like(acc)
    tops[...] = jnp.full_like(tops, NEG)

    loads[0].wait()
    second = (group_ref[0] != 0).astype(jnp.int32)
    by_group[0] = kv_own[second].reshape(N_SEQ // 2, PIECE, 2 * HD)
    by_group[1] = kv_own[1 - second].reshape(N_SEQ // 2, PIECE, 2 * HD)

    def page(owner, source):
        return copy(
            by_group.at[owner // 16, lax.rem(owner, 16)], pages.at[source],
            page_send.at[owner], page_recv.at[source], {"seq": owner, "tp": tp},
        )

    loads[2].wait()
    hid = jnp.concatenate([hid_ref[i].astype(F32) for i in range(hid_ref.shape[0])], axis=0)
    squares = jnp.sum(hid * hid, axis=-1, keepdims=True)
    scaled_in = (hid * gain_ref[...]).astype(BF16)
    part = jnp.dot(scaled_in, wqkv[...], preferred_element_type=F32)
    proj_row[2 * y + k] = jnp.concatenate([part, jnp.broadcast_to(squares, (8, HD))], axis=1)
    loads[1].wait()

    def chunk(zp, yp, zc, ssem, dev, to_mate=False):
        ref = blocks.at[zp, yp, zc, k]
        return copy(ref, ref, ssem, (chip_recv if to_mate else chunk_recv).at[zp, yp, zc], dev)

    def to_mate(zp, yp, zc):
        return chunk(zp, yp, zc, chip_send.at[zp, yp, zc], mate, True)

    def first(zp, direction, zc):
        return chunk(zp, y, zc, first_send.at[zp, direction, zc], (up, down)[direction])

    y_minus, y_plus, y_far = lax.rem(y + 3, NY), lax.rem(y + 1, NY), lax.rem(y + 2, NY)

    def forward(zp, direction):
        return chunk(zp, (y_minus, y_plus)[direction], direction, forward_send.at[zp, direction], (up, down)[direction])

    def far(prompt):
        return copy(
            kv_ref.at[prompt], blocks.at[0, y, s, k], far_send.at[prompt], chunk_recv.at[0, y, s], on(2 + prompt, y, k)
        )

    def arrived(zp, yp, zc):
        chunk(zp, yp, zc, chip_send.at[0, 0, 0], mate).wait_recv()

    def mate_arrived(zp, yp, zc):
        ref = blocks.at[zp, yp, zc, other]
        copy(ref, ref, chip_send.at[0, 0, 0], chip_recv.at[zp, yp, zc], mate).wait_recv()

    def hand_out(zp, zc):
        first(zp, 0, zc).start()
        first(zp, 1, zc).start()
        to_mate(zp, y, zc).start()

    def pass_on(zp, direction):
        yp = (y_minus, y_plus)[direction]
        arrived(zp, yp, direction)
        forward(zp, direction).start()
        to_mate(zp, yp, direction).start()

    def take(zp, yp, zc):
        arrived(zp, yp, zc)
        to_mate(zp, yp, zc).start()

    swap_kv = copy(
        kv_ref.at[1 - s], blocks.at[big, y, s, k], swap_send.at[0], chunk_recv.at[big, y, s], pair
    )
    swap_q = copy(q_ref.at[1 - s], q_in, swap_send.at[1], swap_recv.at[0], pair)

    pl.semaphore_wait(barrier, N_TP + N_SEQ - 2)

    swap_kv.start()
    hand_out(big, s)

    @pl.when(big == 0)
    def _():
        far(0).start()
        far(1).start()

    swap_q.start()
    own_page = pltpu.make_async_copy(by_group.at[seq // 16, lax.rem(seq, 16)], pages.at[seq], local.at[5])
    own_page.start()

    def spread(buf, peer, mine, n_peers, sends, first, recv):
        for d in range(1, n_peers + 1):
            copy(buf.at[mine], buf.at[mine], sends.at[first + d - 1], recv.at[mine], peer(d)).start()

    def gathered(buf, peer, mine, n_peers, sends, first, recv):
        for d in range(1, n_peers + 1):
            src = lax.rem(mine + d, n_peers + 1)
            c = copy(buf.at[src], buf.at[src], sends.at[first + d - 1], recv.at[src], peer(d))
            c.wait()

    spread(proj_row, row_peer, 2 * y + k, ROW - 1, peer_send, 0, pr_recv)

    def scale_queries(ref, r):
        c = math.log2(math.e) / math.sqrt(HD)
        for h in range(HEADS):
            wide = ref[:, h * HD : (h + 1) * HD].astype(F32) * c
            top = wide.astype(BF16)
            q_scaled[r, h] = jnp.concatenate([top, (wide - top.astype(F32)).astype(BF16)], axis=1)

    length = lens_ref[s]

    def attend(r, rows, bias):
        n = rows.shape[0]
        keys, values = rows[:, :HD], rows[:, HD:]
        keys = jnp.concatenate([keys, keys], axis=1)
        values = jnp.concatenate([values, jnp.ones((n, HD), BF16)], axis=1)

        def scores(h):
            return lax.dot_general(q_scaled[r, h], keys, NT, preferred_element_type=F32) + bias

        now_scores = scores(0)
        for h in range(HEADS):
            ahead = scores(h + 1) if h + 1 < HEADS else None
            before = tops[r, h]
            now = jnp.maximum(before, jnp.max(now_scores, axis=-1, keepdims=True))
            p = jnp.exp2(now_scores - jnp.concatenate([now] * (n // HD), axis=1)).astype(BF16)
            shrink = jnp.exp2(before - now)
            tops[r, h] = now
            o = jnp.dot(p, values, preferred_element_type=F32)
            acc[r, h] = acc[r, h] * jnp.concatenate([shrink, shrink], axis=1) + o
            now_scores = ahead

    def near_step(r, yp, zc):
        key_at = ((2 * big + zc) * NY + yp) * BLOCK
        row_at = ((2 * big + r) * NY + y) * BLOCK + k * ROWS
        row = row_at + lax.broadcasted_iota(jnp.int32, (ROWS, BLOCK), 0)
        col = key_at + lax.broadcasted_iota(jnp.int32, (ROWS, BLOCK), 1)
        bias = jnp.where(col < jnp.minimum(row + 1, length), 0.0, NEG)
        attend(r, blocks[big, yp, zc].reshape(BLOCK, 2 * HD), bias)

    def far_step(r, yp):
        attend(r, blocks[0, yp].reshape(2 * BLOCK, 2 * HD), 0.0)

    lane = lax.broadcasted_iota(jnp.int32, (32, HD), 1)

    def packed(top, sums):
        return jnp.where(lane < HD // 2, top, sums)

    def merge(buf, n):
        m = [buf[i, 1][:, :1] for i in range(n)]
        l = [buf[i, 1][:, HD - 1 :] for i in range(n)]
        top = functools.reduce(jnp.maximum, m)
        w = [jnp.exp(t - top) for t in m]
        sums = sum(a * b for a, b in zip(l, w))
        o = sum(buf[i, 0] * w[i] for i in range(n))
        return top, sums, o

    def tree(buf, n):
        parts = [buf[i] for i in range(n)]
        while len(parts) > 1:
            parts = [parts[i] + parts[i + 1] for i in range(0, len(parts), 2)]
        return parts[0]

    def decode_1():
        gathered(proj_row, row_peer, 2 * y + k, ROW - 1, peer_send, 0, pr_recv)
        proj_z[z] = tree(proj_row, ROW)
        spread(proj_z, z_peer, z, 3, peer_send, 7, pz_recv)

    def decode_2():
        gathered(proj_z, z_peer, z, 3, peer_send, 7, pz_recv)
        total = tree(proj_z, NZ)
        proj = total[:, : 6 * HD] * lax.rsqrt(total[:, 6 * HD :][:, :1] / width + EPS)
        sub = lax.broadcasted_iota(jnp.int32, (8, HD), 0)
        position = jnp.where(sub % 2 == 0, lens_ref[0], lens_ref[1]) + sub // 2
        angle = position.astype(F32) * freq_ref[...]
        cosine, sine = jnp.cos(angle), jnp.sin(angle)
        sine = jnp.where(lax.broadcasted_iota(jnp.int32, (8, HD), 1) < HD // 2, -sine, sine)

        def rotated(v):
            return (v * cosine + pltpu.roll(v, HD // 2, 1) * sine).astype(BF16)

        queries = jnp.concatenate([rotated(proj[:, h * HD : (h + 1) * HD]) for h in range(HEADS)], axis=0)
        blank = jnp.zeros((HD - 8, HD), F32)
        new_key = jnp.concatenate([rotated(proj[:, 4 * HD : 5 * HD]).astype(F32), blank], axis=0).astype(BF16)
        new_value = jnp.concatenate([proj[:, 5 * HD : 6 * HD], blank], axis=0).astype(BF16)
        own = kv_own[...].reshape(2 * ROWS, 2 * HD)
        keys = jnp.concatenate([own[:, :HD], new_key], axis=0)
        values = jnp.concatenate([own[:, HD:], new_value], axis=0)
        scores = lax.dot_general(queries, keys, NT, preferred_element_type=F32) * (1.0 / math.sqrt(HD))
        row = lax.broadcasted_iota(jnp.int32, scores.shape, 0) % 8
        col = lax.broadcasted_iota(jnp.int32, scores.shape, 1)
        new = col - 2 * ROWS
        limit = jnp.where(col < ROWS, lens_ref[0], lens_ref[1])
        old_ok = (col < 2 * ROWS) & (col // ROWS == row % 2) & (seq * ROWS + col % ROWS < limit)
        new_ok = (new >= 0) & (new <= row) & (new % 2 == row % 2) & (seq == 0)
        scores = jnp.where(old_ok | new_ok, scores, NEG)
        top = jnp.max(scores, axis=-1, keepdims=True)
        p = jnp.exp(scores - top)
        mine = 2 * y + k
        soft_row[mine, 0] = jnp.dot(p.astype(BF16), values, preferred_element_type=F32)
        soft_row[mine, 1] = packed(top, jnp.sum(p, axis=-1, keepdims=True))
        spread(soft_row, row_peer, mine, ROW - 1, peer_send, 10, sr_recv)

    def decode_3():
        gathered(soft_row, row_peer, 2 * y + k, ROW - 1, peer_send, 10, sr_recv)
        top, sums, o = merge(soft_row, ROW)
        soft_z[z, 0] = o
        soft_z[z, 1] = packed(top, sums)
        spread(soft_z, z_peer, z, 3, peer_send, 17, sz_recv)

    def decode_4():
        gathered(soft_z, z_peer, z, 3, peer_send, 17, sz_recv)
        _, sums, o = merge(soft_z, NZ)
        att = o / sums
        out = jnp.zeros((8, ROWS), F32)
        for h in range(HEADS):
            head = att[8 * h : 8 * h + 8].astype(BF16)
            out += jnp.dot(head, wout[h * HD : (h + 1) * HD, :], preferred_element_type=F32)
        out_tp[tp] = out
        spread(out_tp, tp_peer, tp, N_TP - 1, peer_send, 20, ot_recv)

    def decode_5():
        gathered(out_tp, tp_peer, tp, N_TP - 1, peer_send, 20, ot_recv)
        dec_ref[...] = (hid + tree(out_tp, N_TP)).astype(BF16)

    def far_first(zc):
        @pl.when(big == 1)
        def _():
            arrived(0, y, zc)
            hand_out(0, zc)

    def far_pass_on():
        @pl.when(big == 1)
        def _():
            pass_on(0, 0)
            pass_on(0, 1)

    def far_take(*which):
        @pl.when(big == 1)
        def _():
            for yp, zc in which:
                take(0, yp, zc)

    loads[3].wait()
    scale_queries(q_own, s)

    def by(i, values):
        out = values[-1]
        for j in range(len(values) - 2, -1, -1):
            out = jnp.where(i == j, values[j], out)
        return out

    def result(r, h):
        return (acc[r, h][:, :HD] / acc[r, h][:, HD:]).astype(BF16)

    back = copy(o_out, o_in, swap_send.at[2], swap_recv.at[1], pair)

    near_2 = 8 + EARLY
    far_2 = near_2 + 8
    far_3 = far_2 + NY

    @pl.loop(0, far_3 + NY - EARLY)
    def _(i):
        @pl.when(i == 1)
        def _():
            arrived(big, y, 1 - s)
            hand_out(big, 1 - s)

        @pl.when(i == 2)
        def _():
            pass_on(big, 0)
            pass_on(big, 1)

        @pl.when(i == 4)
        def _():
            take(big, y_minus, 1)
            take(big, y_plus, 0)
            far_first(s)
            decode_1()

        @pl.when(i == 6)
        def _():
            take(big, y_far, 0)
            take(big, y_far, 1)
            far_first(1 - s)

        @pl.when(i == 8)
        def _():
            decode_2()

            @pl.loop(1, N_SEQ)
            def _(d):
                page(lax.rem(seq + d, N_SEQ), seq).start()

        @pl.when(i == near_2)
        def _():
            far_pass_on()
            swap_q.wait_recv()
            scale_queries(q_in, 1 - s)

        @pl.when(i == near_2 + 2)
        def _():
            far_take((y_minus, 1), (y_plus, 0))

        @pl.when(i == near_2 + 4)
        def _():
            decode_3()

        @pl.when(i == near_2 + 6)
        def _():
            far_take((y_far, 0), (y_far, 1))

        @pl.when(i == far_2 + 1)
        def _():
            loads[4].wait()
            decode_4()

        @pl.when(i == far_3)
        def _():
            for h in range(HEADS):
                o_out[:, h * HD : (h + 1) * HD] = result(1 - s, h)
            back.start()

        j = jnp.where(i < 8, i, i - near_2)
        yp = lax.rem(y + by(j, [0, 0, 3, 1, 3, 1, 2, 2]), NY)
        zc = by(j, [s, 1 - s, 0, 1, 1, 0, 0, 1])
        r = jnp.where(i < 8, s, 1 - s)

        @pl.when(i < 8)
        def _():
            mate_arrived(big, yp, zc)

        @pl.when((i < 8) | ((i >= near_2) & (i < far_2)))
        def _():
            @pl.when(zc * NY + yp <= r * NY + y)
            def _():
                near_step(r, yp, zc)

        place = jnp.where(i < near_2, i - 8, jnp.where(i < far_3, i - far_2, i - far_3 + EARLY))
        far_yp = lax.rem(y + by(place, [0, 3, 1, 2]), NY)
        again = (i >= far_2) & (i < far_2 + EARLY) | (i >= far_3)
        early = (i >= 8) & (i < near_2)

        @pl.when((big == 1) & (early | (i >= far_2)))
        def _():
            @pl.when(jnp.logical_not(again))
            def _():
                mate_arrived(0, far_yp, 0)
                mate_arrived(0, far_yp, 1)

            far_step(jnp.where((i >= far_2) & (i < far_3), 1 - s, s), far_yp)

    for h in range(HEADS):
        o_own[:, h * HD : (h + 1) * HD] = result(s, h)
    stores = [
        pltpu.make_async_copy(src, dst, local.at[i])
        for i, (src, dst) in enumerate([(o_own, attn_ref.at[s]), (pages, pages_ref), (o_in, attn_ref.at[1 - s])])
    ]
    stores[0].start()
    decode_5()

    swap_kv.wait_send()
    swap_q.wait_send()
    own_page.wait()

    @pl.loop(1, N_SEQ)
    def _(d):
        page(lax.rem(seq + d, N_SEQ), lax.rem(seq + d, N_SEQ)).wait()

    stores[1].start()

    @pl.loop(0, 2)
    def _(zp):
        @pl.when(zp <= big)
        def _():
            for zc in (0, 1):
                for direction in (0, 1):
                    first(zp, direction, zc).wait_send()
                for yp in range(NY):
                    to_mate(zp, yp, zc).wait_send()
                forward(zp, zc).wait_send()

    @pl.when(big == 0)
    def _():
        far(0).wait_send()
        far(1).wait_send()

    back.wait()
    stores[2].start()
    for store in stores:
        store.wait()


def publish(attn_ref, pages_ref, dec_ref, attn_out, pages_out, dec_out, attn, pages, arrive, leave):
    pieces = [
        (attn_ref.at[p, pl.ds(r, HD)], attn.at[p, pl.ds(r, HD)], attn_out.at[p, pl.ds(r, HD)]) for p in (0, 1) for r in (0, HD)
    ]
    half = N_SEQ // 2
    pieces += [(pages_ref.at[pl.ds(r, half)], pages.at[pl.ds(r, half)], pages_out.at[pl.ds(r, half)]) for r in (0, half)]
    inward = [pltpu.make_async_copy(src, via, arrive.at[i]) for i, (src, via, _) in enumerate(pieces)]
    outward = [pltpu.make_async_copy(via, dst, leave.at[i]) for i, (_, via, dst) in enumerate(pieces)]
    for c in inward:
        c.start()
    for i in range(dec_out.shape[0]):
        dec_out[i] = dec_ref[2 * i : 2 * i + 2, :]
    for c, then in zip(inward, outward):
        c.wait()
        then.start()
    for c in outward:
        c.wait()


def on_device(q_prefill, kv_prefill, prompt_len, group_of, hidden, norm_gain, w_qkv, w_out):
    n_prompts, rows = q_prefill.shape[:2]
    cycle = lax.axis_size("seq")
    steps = hidden.shape[0]
    frequency = BASE ** (-2.0 * np.arange(HD // 2, dtype=np.float64) / HD)
    frequency = np.concatenate([frequency, frequency])[None].astype(np.float32)

    vmem = pl.BlockSpec(memory_space=pltpu.VMEM)
    smem = pl.BlockSpec(memory_space=pltpu.SMEM)
    hbm = pl.BlockSpec(memory_space=pltpu.HBM)
    dma = pltpu.SemaphoreType.DMA
    width = hidden.shape[2] * cycle
    attn, pages, decoded = pl.pallas_call(
        functools.partial(kernel, float(width)),
        out_shape=(
            jax.ShapeDtypeStruct((n_prompts, rows, HEADS * HD), BF16),
            jax.ShapeDtypeStruct((N_SEQ, PIECE, 2 * HD), BF16),
            jax.ShapeDtypeStruct((steps * n_prompts, rows), BF16),
        ),
        in_specs=[smem, smem, hbm, hbm, vmem, vmem, hbm, hbm, vmem],
        out_specs=(hbm, hbm, vmem),
        scratch_shapes=[
            pltpu.VMEM((2, NY, 2, 2, ROWS, 2 * HD), BF16),
            pltpu.VMEM((2, ROWS, 2 * HD), BF16),
            pltpu.VMEM((ROWS, HEADS * HD), BF16),
            pltpu.VMEM((ROWS, HEADS * HD), BF16),
            pltpu.VMEM((ROWS, 6 * HD), BF16),
            pltpu.VMEM((HEADS * HD, ROWS), BF16),
            pltpu.VMEM((2, HEADS, ROWS, 2 * HD), BF16),
            pltpu.VMEM((2, HEADS, ROWS, 2 * HD), F32),
            pltpu.VMEM((2, HEADS, ROWS, HD), F32),
            pltpu.VMEM((ROWS, HEADS * HD), BF16),
            pltpu.VMEM((ROWS, HEADS * HD), BF16),
            pltpu.VMEM((ROWS, HEADS * HD), BF16),
            pltpu.VMEM((ROW, 8, 7 * HD), F32),
            pltpu.VMEM((NZ, 8, 7 * HD), F32),
            pltpu.VMEM((ROW, 2, 32, HD), F32),
            pltpu.VMEM((NZ, 2, 32, HD), F32),
            pltpu.VMEM((N_TP, 8, ROWS), F32),
            pltpu.VMEM((2, N_SEQ // 2, PIECE, 2 * HD), BF16),
            pltpu.VMEM((N_SEQ, PIECE, 2 * HD), BF16),
            dma((6,)), dma((3,)), dma((2,)), dma((2, NY, 2)), dma((2, NY, 2)),
            dma((2, 2, 2)), dma((2, 2)), dma((2, NY, 2)), dma((2,)),
            dma((27,)), dma((ROW,)), dma((NZ,)), dma((ROW,)), dma((NZ,)), dma((N_TP,)),
            dma((N_SEQ,)), dma((N_SEQ,)),
        ],
        compiler_params=pltpu.CompilerParams(
            collective_id=0, has_side_effects=True, vmem_limit_bytes=62 * 1024 * 1024
        ),
        cost_estimate=pl.CostEstimate(flops=9 * 10**9, bytes_accessed=3 * 10**6, transcendentals=17 * 10**6),
    )(
        prompt_len,
        group_of,
        q_prefill.reshape(n_prompts, rows, HEADS * HD),
        kv_prefill.reshape(n_prompts, rows, 2 * HD),
        hidden,
        norm_gain.reshape(1, rows),
        w_qkv.reshape(rows, 6 * HD),
        w_out.reshape(HEADS * HD, rows),
        frequency,
    )
    attn, pages, decoded = pl.pallas_call(
        publish,
        out_shape=(
            jax.ShapeDtypeStruct(attn.shape, BF16),
            jax.ShapeDtypeStruct(pages.shape, BF16),
            jax.ShapeDtypeStruct(hidden.shape, BF16),
        ),
        in_specs=[hbm, hbm, vmem],
        out_specs=(hbm, hbm, vmem),
        scratch_shapes=[pltpu.VMEM(attn.shape, BF16), pltpu.VMEM(pages.shape, BF16), dma((6,)), dma((6,))],
        compiler_params=pltpu.CompilerParams(vmem_limit_bytes=62 * 1024 * 1024),
    )(attn, pages, decoded)
    return (
        attn.reshape(n_prompts, rows, 1, HEADS * HD),
        pages.reshape(N_SEQ * PIECE, 1, 2 * HD),
        decoded,
    )


def solution(mesh):
    placed = (
        P(None, "seq", "tp", None),
        P(None, "seq", "tp", None),
        P(),
        P(),
        P(None, None, "seq"),
        P("seq"),
        P("seq", "tp", None),
        P("tp", None, "seq"),
    )
    return jax.shard_map(
        on_device,
        mesh=mesh,
        in_specs=placed,
        out_specs=(P(None, "seq", "tp", None), P("seq", "tp", None), P(None, None, "seq")),
        check_vma=False,
    )
```

time: 862 us -> 62 us (0.07); the launches traced: 848 us -> 61.8 us
  blocking collectives: 622 us -> 0 us
  matrix products: 80.3 us -> 0 us
  other arithmetic: 74.2 us -> 0 us
  Pallas kernels: 0 us -> 61.2 us
  local copies, waits for them, and re-layouts: 41.7 us -> 0 us
  between operations: 14.4 us -> 0.64 us
    all_gather x12 -> x0, blocking collectives: 484 us -> none  [merged(): everything = jax.tree.map(lambda part: lax.all_gather(part, axis), shard)]
    psum x2 -> x0, blocking collectives: 138 us -> none  [the longest x1 107 us: on_device(): squares, partial_proj = lax.psum((squares, partial_proj), 'seq')]
    dot_general x39 -> x0, matrix products: 80.3 us -> none  [the longest x8 37.5 us: key_step(): jnp.einsum('prhqd,pnhd->prhqn', queries, key_block[..., :head_size], pref...]
    pallas_call x0 -> x2, Pallas kernels: none -> 61.2 us  [the longest x1 57.9 us: on_device(): pl.pallas_call(functools.partial(kernel, float(width)), out_shape=(jax.Sh...]
    reduce_sum x14 -> x0, other arithmetic: 43.7 us -> none  [the longest x8 41.8 us: key_step(): row_total = row_total * shrink + jnp.sum(weight_matrices, axis=-1)]
    while x212 -> x0, local copies, waits for them, and re-layouts: 14.7 us -> none
    add x150 -> x0, other arithmetic: 10.9 us -> none  [the longest x124 10.6 us: combine_parts(): earlier[2] * earlier_scale[..., None] + later[2] * later_scale[..., None]]
    squeeze x16 -> x0, local copies, waits for them, and re-layouts: 10.4 us -> none  [the longest x8 10.4 us: on_device(): lax.scan(key_step, running, (blocks, jnp.arange(block_total, dtype=jnp.in...]
  transfers between devices with their start and end apart: 2 -> 0, of which waited for: 0 -> 0; matrix products, arithmetic and copies ran while one was open for 4% -> 0% of each run, Pallas kernels for 0% -> 0%
where the time goes in v3:
time: 62 us; the launch traced here: 61.8 us
  Pallas kernels  61.2 us (99%)
  between operations  0.64 us (1%)
    pallas_call x1, Pallas kernels, on_device(): pl.pallas_call(functools.partial(kernel, float(width)), out_shape=(jax.Sh...  57.9 us
    pallas_call x1, Pallas kernels, on_device(): pl.pallas_call(publish, out_shape=(jax.ShapeDtypeStruct(attn.shape, BF16)...  3.23 us

profile of v3, /device:TPU:64, one launch (start us, length us, event | category | flops | bytes accessed | tf_op | source)
XLA Modules:
  0.0 61.8 jit_solution(14059168747232192023)
XLA Ops:
  0.6 57.9 %shard_map.112 = (bf16[2,256,512]{2,1,0:T(8,128)(2,1)}, bf16[32,16,256]{2,1,0:T(8,128)(2,1)}, bf16[8,256]{1,0:T(8,128)(2,1)}) custom-call(s32[2]{0:T(128)} %lens_ref.1, s32[2]{0:T(128)} %group_ref.1, bf16[2,256,512]{2,1,0:T(8,128)(2,1)} %bitcast.9, bf16[2,256,256]{2,1,0:T(8,128)(2,1)} %bitcast.12, bf16[4,2,256]{2,1,0:T(2,128)(2,1)} %hid_ref.1, ...), custom_call_target="tpu_custom_call" | custom-call | flops 8999999488 | bytes 3000000 | tf_op jit(solution)/shard_map/pallas_call | solution.py:509
  58.6 3.2 %shard_map.113 = (bf16[2,256,512]{2,1,0:T(8,128)(2,1)}, bf16[32,16,256]{2,1,0:T(8,128)(2,1)}, bf16[4,2,256]{2,1,0:T(2,128)(2,1)}) custom-call(bf16[2,256,512]{2,1,0:T(8,128)(2,1)} %get-tuple-element.9.attn_ref, bf16[32,16,256]{2,1,0:T(8,128)(2,1)} %get-tuple-element.10.pages_ref, bf16[8,256]{1,0:T(8,128)(2,1)} %get-tuple-element.11.dec_ref), custom_call_target="tpu_custom_call" | custom-call | tf_op jit(solution)/shard_map/pallas_call | solution.py:558

commit v4 on v3

--- a/solution.py
+++ b/solution.py
@@ -21,7 +21,7 @@
 NZ = 4
 ROW = 8
 N_TP = 8
-EARLY = 1
+EARLY = 0
 N_SEQ = 32
 PIECE = 16
 BF16 = jnp.bfloat16
@@ -33,7 +33,7 @@
     width,
     lens_ref, group_ref, q_ref, kv_ref, hid_ref, gain_ref, wqkv_ref, wout_ref, freq_ref,
     attn_ref, pages_ref, dec_ref,
-    blocks, kv_own, q_own, q_in, wqkv, wout, q_scaled, acc, tops, o_in, o_out, o_own,
+    blocks, kv_own, q_own, q_in, wqkv, wout, q_scaled, acc, tops, o_in, o_out,
     proj_row, proj_z, soft_row, soft_z, out_tp, by_group, pages,
     local, swap_send, swap_recv, chunk_recv, chip_recv,
     first_send, forward_send, chip_send, far_send,
@@ -435,12 +435,7 @@
             far_step(jnp.where((i >= far_2) & (i < far_3), 1 - s, s), far_yp)
 
     for h in range(HEADS):
-        o_own[:, h * HD : (h + 1) * HD] = result(s, h)
-    stores = [
-        pltpu.make_async_copy(src, dst, local.at[i])
-        for i, (src, dst) in enumerate([(o_own, attn_ref.at[s]), (pages, pages_ref), (o_in, attn_ref.at[1 - s])])
-    ]
-    stores[0].start()
+        attn_ref[s, :, h * HD : (h + 1) * HD] = result(s, h)
     decode_5()
 
     swap_kv.wait_send()
@@ -451,7 +446,7 @@
     def _(d):
         page(lax.rem(seq + d, N_SEQ), lax.rem(seq + d, N_SEQ)).wait()
 
-    stores[1].start()
+    pages_ref[...] = pages[...]
 
     @pl.loop(0, 2)
     def _(zp):
@@ -470,26 +465,16 @@
         far(1).wait_send()
 
     back.wait()
-    stores[2].start()
-    for store in stores:
-        store.wait()
-
-
-def publish(attn_ref, pages_ref, dec_ref, attn_out, pages_out, dec_out, attn, pages, arrive, leave):
-    pieces = [
-        (attn_ref.at[p, pl.ds(r, HD)], attn.at[p, pl.ds(r, HD)], attn_out.at[p, pl.ds(r, HD)]) for p in (0, 1) for r in (0, HD)
-    ]
-    half = N_SEQ // 2
-    pieces += [(pages_ref.at[pl.ds(r, half)], pages.at[pl.ds(r, half)], pages_out.at[pl.ds(r, half)]) for r in (0, half)]
-    inward = [pltpu.make_async_copy(src, via, arrive.at[i]) for i, (src, via, _) in enumerate(pieces)]
-    outward = [pltpu.make_async_copy(via, dst, leave.at[i]) for i, (_, via, dst) in enumerate(pieces)]
-    for c in inward:
+    attn_ref[1 - s] = o_in[...]
+
+
+def publish(attn_ref, pages_ref, dec_ref, attn_out, pages_out, dec_out, leave):
+    pieces = [(attn_ref.at[0], attn_out.at[0]), (attn_ref.at[1], attn_out.at[1]), (pages_ref, pages_out)]
+    outward = [pltpu.make_async_copy(src, dst, leave.at[i]) for i, (src, dst) in enumerate(pieces)]
+    for c in outward:
         c.start()
     for i in range(dec_out.shape[0]):
         dec_out[i] = dec_ref[2 * i : 2 * i + 2, :]
-    for c, then in zip(inward, outward):
-        c.wait()
-        then.start()
     for c in outward:
         c.wait()
 
@@ -509,12 +494,12 @@
     attn, pages, decoded = pl.pallas_call(
         functools.partial(kernel, float(width)),
         out_shape=(
-            jax.ShapeDtypeStruct((n_prompts, rows, HEADS * HD), BF16),
-            jax.ShapeDtypeStruct((N_SEQ, PIECE, 2 * HD), BF16),
-            jax.ShapeDtypeStruct((steps * n_prompts, rows), BF16),
+            pltpu.VMEM((n_prompts, rows, HEADS * HD), BF16),
+            pltpu.VMEM((N_SEQ, PIECE, 2 * HD), BF16),
+            pltpu.VMEM((steps * n_prompts, rows), BF16),
         ),
         in_specs=[smem, smem, hbm, hbm, vmem, vmem, hbm, hbm, vmem],
-        out_specs=(hbm, hbm, vmem),
+        out_specs=(vmem, vmem, vmem),
         scratch_shapes=[
             pltpu.VMEM((2, NY, 2, 2, ROWS, 2 * HD), BF16),
             pltpu.VMEM((2, ROWS, 2 * HD), BF16),
@@ -525,7 +510,6 @@
             pltpu.VMEM((2, HEADS, ROWS, 2 * HD), BF16),
             pltpu.VMEM((2, HEADS, ROWS, 2 * HD), F32),
             pltpu.VMEM((2, HEADS, ROWS, HD), F32),
-            pltpu.VMEM((ROWS, HEADS * HD), BF16),
             pltpu.VMEM((ROWS, HEADS * HD), BF16),
             pltpu.VMEM((ROWS, HEADS * HD), BF16),
             pltpu.VMEM((ROW, 8, 7 * HD), F32),
@@ -541,7 +525,7 @@
             dma((N_SEQ,)), dma((N_SEQ,)),
         ],
         compiler_params=pltpu.CompilerParams(
-            collective_id=0, has_side_effects=True, vmem_limit_bytes=62 * 1024 * 1024
+            collective_id=0, has_side_effects=True, vmem_limit_bytes=60 * 1024 * 1024
         ),
         cost_estimate=pl.CostEstimate(flops=9 * 10**9, bytes_accessed=3 * 10**6, transcendentals=17 * 10**6),
     )(
@@ -562,10 +546,10 @@
             jax.ShapeDtypeStruct(pages.shape, BF16),
             jax.ShapeDtypeStruct(hidden.shape, BF16),
         ),
-        in_specs=[hbm, hbm, vmem],
+        in_specs=[vmem, vmem, vmem],
         out_specs=(hbm, hbm, vmem),
-        scratch_shapes=[pltpu.VMEM(attn.shape, BF16), pltpu.VMEM(pages.shape, BF16), dma((6,)), dma((6,))],
-        compiler_params=pltpu.CompilerParams(vmem_limit_bytes=62 * 1024 * 1024),
+        scratch_shapes=[dma((3,))],
+        compiler_params=pltpu.CompilerParams(vmem_limit_bytes=16 * 1024 * 1024),
     )(attn, pages, decoded)
     return (
         attn.reshape(n_prompts, rows, 1, HEADS * HD),

time: 62 us -> 58.9 us (0.950)
  Pallas kernels: 61.2 us -> 58.1 us
    pallas_call x1, Pallas kernels: 3.23 us -> 1.5 us  [on_device(): pl.pallas_call(publish, out_shape=(jax.ShapeDtypeStruct(attn.shape, BF16)...]
    pallas_call x1, Pallas kernels: 57.9 us -> 56.6 us  [on_device(): pl.pallas_call(functools.partial(kernel, float(width)), out_shape=(pltpu....]
where the time goes in v4:
time: 58.9 us; the launch traced here: 58.8 us
  Pallas kernels  58.1 us (99%)
  between operations  0.64 us (1%)
    pallas_call x1, Pallas kernels, on_device(): pl.pallas_call(functools.partial(kernel, float(width)), out_shape=(pltpu....  56.6 us
    pallas_call x1, Pallas kernels, on_device(): pl.pallas_call(publish, out_shape=(jax.ShapeDtypeStruct(attn.shape, BF16)...  1.5 us

profile of v4, /device:TPU:64, one launch (start us, length us, event | category | flops | bytes accessed | tf_op | source)
XLA Modules:
  0.0 58.8 jit_solution(15346812677775594482)
XLA Ops:
  0.6 56.6 %shard_map.112 = (bf16[2,256,512]{2,1,0:T(8,128)(2,1)S(1)}, bf16[32,16,256]{2,1,0:T(8,128)(2,1)S(1)}, bf16[8,256]{1,0:T(8,128)(2,1)S(1)}) custom-call(s32[2]{0:T(128)} %lens_ref.1, s32[2]{0:T(128)} %group_ref.1, bf16[2,256,512]{2,1,0:T(8,128)(2,1)} %bitcast.9, bf16[2,256,256]{2,1,0:T(8,128)(2,1)} %bitcast.12, bf16[4,2,256]{2,1,0:T(2,128)(2,1)} %hid_ref.1, ...), custom_call_target="tpu_custom_call" | custom-call | flops 8999999488 | bytes 3000000 | tf_op jit(solution)/shard_map/pallas_call | solution.py:494
  57.3 1.5 %shard_map.113 = (bf16[2,256,512]{2,1,0:T(8,128)(2,1)}, bf16[32,16,256]{2,1,0:T(8,128)(2,1)}, bf16[4,2,256]{2,1,0:T(2,128)(2,1)}) custom-call(bf16[2,256,512]{2,1,0:T(8,128)(2,1)S(1)} %get-tuple-element.9.attn_ref, bf16[32,16,256]{2,1,0:T(8,128)(2,1)S(1)} %get-tuple-element.10.pages_ref, bf16[8,256]{1,0:T(8,128)(2,1)S(1)} %get-tuple-element.11.dec_ref), custom_call_target="tpu_custom_call" | custom-call | tf_op jit(solution)/shard_map/pallas_call | solution.py:542

commit v5 on v4

--- a/solution.py
+++ b/solution.py
@@ -158,38 +158,40 @@
     )
     swap_q = copy(q_ref.at[1 - s], q_in, swap_send.at[1], swap_recv.at[0], pair)
 
-    pl.semaphore_wait(barrier, N_TP + N_SEQ - 2)
-
-    swap_kv.start()
-    hand_out(big, s)
-
-    @pl.when(big == 0)
-    def _():
-        far(0).start()
-        far(1).start()
-
-    swap_q.start()
-    own_page = pltpu.make_async_copy(by_group.at[seq // 16, lax.rem(seq, 16)], pages.at[seq], local.at[5])
-    own_page.start()
-
-    def spread(buf, peer, mine, n_peers, sends, first, recv):
-        for d in range(1, n_peers + 1):
-            copy(buf.at[mine], buf.at[mine], sends.at[first + d - 1], recv.at[mine], peer(d)).start()
-
-    def gathered(buf, peer, mine, n_peers, sends, first, recv):
-        for d in range(1, n_peers + 1):
-            src = lax.rem(mine + d, n_peers + 1)
-            c = copy(buf.at[src], buf.at[src], sends.at[first + d - 1], recv.at[src], peer(d))
-            c.wait()
-
-    spread(proj_row, row_peer, 2 * y + k, ROW - 1, peer_send, 0, pr_recv)
-
     def scale_queries(ref, r):
         c = math.log2(math.e) / math.sqrt(HD)
         for h in range(HEADS):
             wide = ref[:, h * HD : (h + 1) * HD].astype(F32) * c
             top = wide.astype(BF16)
             q_scaled[r, h] = jnp.concatenate([top, (wide - top.astype(F32)).astype(BF16)], axis=1)
+
+    loads[3].wait()
+    scale_queries(q_own, s)
+    pl.semaphore_wait(barrier, N_TP + N_SEQ - 2)
+
+    swap_kv.start()
+    hand_out(big, s)
+
+    @pl.when(big == 0)
+    def _():
+        far(0).start()
+        far(1).start()
+
+    swap_q.start()
+    own_page = pltpu.make_async_copy(by_group.at[seq // 16, lax.rem(seq, 16)], pages.at[seq], local.at[5])
+    own_page.start()
+
+    def spread(buf, peer, mine, n_peers, sends, first, recv):
+        for d in range(1, n_peers + 1):
+            copy(buf.at[mine], buf.at[mine], sends.at[first + d - 1], recv.at[mine], peer(d)).start()
+
+    def gathered(buf, peer, mine, n_peers, sends, first, recv):
+        for d in range(1, n_peers + 1):
+            src = lax.rem(mine + d, n_peers + 1)
+            c = copy(buf.at[src], buf.at[src], sends.at[first + d - 1], recv.at[src], peer(d))
+            c.wait()
+
+    spread(proj_row, row_peer, 2 * y + k, ROW - 1, peer_send, 0, pr_recv)
 
     length = lens_ref[s]
 
@@ -325,9 +327,6 @@
             for yp, zc in which:
                 take(0, yp, zc)
 
-    loads[3].wait()
-    scale_queries(q_own, s)
-
     def by(i, values):
         out = values[-1]
         for j in range(len(values) - 2, -1, -1):
@@ -372,27 +371,27 @@
         def _():
             decode_2()
 
+        @pl.when(i == near_2)
+        def _():
+            far_pass_on()
+            swap_q.wait_recv()
+            scale_queries(q_in, 1 - s)
+
+        @pl.when(i == near_2 + 2)
+        def _():
+            far_take((y_minus, 1), (y_plus, 0))
+
+        @pl.when(i == near_2 + 4)
+        def _():
+            decode_3()
+
+        @pl.when(i == near_2 + 6)
+        def _():
+            far_take((y_far, 0), (y_far, 1))
+
             @pl.loop(1, N_SEQ)
             def _(d):
                 page(lax.rem(seq + d, N_SEQ), seq).start()
-
-        @pl.when(i == near_2)
-        def _():
-            far_pass_on()
-            swap_q.wait_recv()
-            scale_queries(q_in, 1 - s)
-
-        @pl.when(i == near_2 + 2)
-        def _():
-            far_take((y_minus, 1), (y_plus, 0))
-
-        @pl.when(i == near_2 + 4)
-        def _():
-            decode_3()
-
-        @pl.when(i == near_2 + 6)
-        def _():
-            far_take((y_far, 0), (y_far, 1))
 
         @pl.when(i == far_2 + 1)
         def _():

time: 58.9 us -> 57.9 us (0.983)
  Pallas kernels: 58.1 us -> 57.2 us
    pallas_call x1, Pallas kernels: 56.6 us -> 55.7 us  [on_device(): pl.pallas_call(functools.partial(kernel, float(width)), out_shape=(pltpu....]
where the time goes in v5:
time: 57.9 us; the launch traced here: 57.8 us
  Pallas kernels  57.2 us (99%)
  between operations  0.64 us (1%)
    pallas_call x1, Pallas kernels, on_device(): pl.pallas_call(functools.partial(kernel, float(width)), out_shape=(pltpu....  55.7 us
    pallas_call x1, Pallas kernels, on_device(): pl.pallas_call(publish, out_shape=(jax.ShapeDtypeStruct(attn.shape, BF16)...  1.5 us

profile of v5, /device:TPU:64, one launch (start us, length us, event | category | flops | bytes accessed | tf_op | source)
XLA Modules:
  0.0 57.8 jit_solution(13309995225537597476)
XLA Ops:
  0.6 55.7 %shard_map.112 = (bf16[2,256,512]{2,1,0:T(8,128)(2,1)S(1)}, bf16[32,16,256]{2,1,0:T(8,128)(2,1)S(1)}, bf16[8,256]{1,0:T(8,128)(2,1)S(1)}) custom-call(s32[2]{0:T(128)} %lens_ref.1, s32[2]{0:T(128)} %group_ref.1, bf16[2,256,512]{2,1,0:T(8,128)(2,1)} %bitcast.9, bf16[2,256,256]{2,1,0:T(8,128)(2,1)} %bitcast.12, bf16[4,2,256]{2,1,0:T(2,128)(2,1)} %hid_ref.1, ...), custom_call_target="tpu_custom_call" | custom-call | flops 8999999488 | bytes 3000000 | tf_op jit(solution)/shard_map/pallas_call | solution.py:493
  56.3 1.5 %shard_map.113 = (bf16[2,256,512]{2,1,0:T(8,128)(2,1)}, bf16[32,16,256]{2,1,0:T(8,128)(2,1)}, bf16[4,2,256]{2,1,0:T(2,128)(2,1)}) custom-call(bf16[2,256,512]{2,1,0:T(8,128)(2,1)S(1)} %get-tuple-element.9.attn_ref, bf16[32,16,256]{2,1,0:T(8,128)(2,1)S(1)} %get-tuple-element.10.pages_ref, bf16[8,256]{1,0:T(8,128)(2,1)S(1)} %get-tuple-element.11.dec_ref), custom_call_target="tpu_custom_call" | custom-call | tf_op jit(solution)/shard_map/pallas_call | solution.py:541
